TPU v7x, 32 devices: a whole 2x2x4 slice. The times are simulated.
32 devices in a mesh: segment: 2 (over core), dp: 8 (over z, y), tensor: 2 (over x).
Axes of the slice: x: 2, y: 2, z: 4, core: 2. Of those that a mesh axis runs over, the one named last changes fastest.
Arguments:
- tokens: bfloat16 [256, 5120], P('dp'), may hold values from -12 to 12
- cotangent: bfloat16 [256, 5120], P('dp'), may hold values from -6 to 6
- gains: float32 [2, 5120], P('segment'), may hold values from 0.1 to 1.9
- w_gate: bfloat16 [2, 5120, 27648], P('segment', 'dp', 'tensor'), may hold values from -0.078125 to 0.078125
- w_up: bfloat16 [2, 5120, 27648], P('segment', 'dp', 'tensor'), may hold values from -0.078125 to 0.078125
- w_down: bfloat16 [2, 5120, 27648], P('segment', 'dp', 'tensor'), may hold values from -0.0390625 to 0.0390625
Outputs:
- acts: bfloat16 [2, 256, 5120], P('segment', 'dp')
- grads: bfloat16 [2, 256, 5120], P('segment', 'dp')
All inputs are finite; a program needn't handle non-finite values.
Results may differ from a plain program's by a relative error of at most 0.04.
Values may be sent and summed in bfloat16 or wider, within the bound.
No kernel may reach another device: no remote copies, remote signals or barrier semaphores. Data moves between devices by JAX's collectives and lax.ppermute only.
A program may use at most 128 MiB of HBM per device.

v0:
```python
import jax
import jax.numpy as jnp
from jax import lax
from jax.sharding import PartitionSpec as P

EPSILON = 1e-06


def from_behind(value, axis, steps):
    count = lax.axis_size(axis)
    leading, last = (max(0, -steps), min(count, count - steps))
    return lax.ppermute(value, axis, [(source, source + steps) for source in range(leading, last)])


def normalize(values):
    wide = values.astype(jnp.float32)
    inverse = lax.rsqrt(jnp.mean(wide * wide, axis=1, keepdims=True) + EPSILON)
    return (wide, wide * inverse, inverse)


def contract_last(left, right):
    return lax.dot_general(
        left, right, (((1,), (1,)), ((), ())), preferred_element_type=jnp.float32
    )


def input_grads(d_hidden, stash_gate, stash_up):
    gate_pre = stash_gate.astype(jnp.float32)
    up_pre = stash_up.astype(jnp.float32)
    sigmoid_gate = jax.nn.sigmoid(gate_pre)
    d_gate = (d_hidden * up_pre * sigmoid_gate * (1.0 + gate_pre * (1.0 - sigmoid_gate))).astype(
        jnp.bfloat16
    )
    d_up = (d_hidden * gate_pre * sigmoid_gate).astype(jnp.bfloat16)
    return (d_gate, d_up)


def norm_back(unit, inverse, gain_row, d_normed, incoming):
    weighted = d_normed * gain_row
    projection = jnp.mean(weighted * unit, axis=1, keepdims=True)
    return (incoming.astype(jnp.float32) + inverse * (weighted - unit * projection)).astype(
        jnp.bfloat16
    )


def unchanged(current):
    return current


def to_columns(rows_here):
    return lax.all_to_all(rows_here, "dp", split_axis=1, concat_axis=0, tiled=True)


def hidden_sums(first_term, second_term):
    return (
        lax.psum_scatter(
            first_term.astype(jnp.bfloat16), "dp", scatter_dimension=1, tiled=True
        ).astype(jnp.float32),
        lax.psum_scatter(
            second_term.astype(jnp.bfloat16), "dp", scatter_dimension=1, tiled=True
        ).astype(jnp.float32),
    )


def sum_back(partial_value, complete):
    own_rows = partial_value.shape[0] // lax.axis_size("dp")
    rows_part = lax.all_to_all(
        partial_value.astype(jnp.bfloat16), "dp", split_axis=0, concat_axis=1, tiled=True
    ).astype(partial_value.dtype)
    share_count = own_rows // lax.axis_size("tensor")
    mine = lax.psum_scatter(
        rows_part.astype(jnp.bfloat16), "tensor", scatter_dimension=0, tiled=True
    ).astype(jnp.float32)
    finished = complete(mine, lax.axis_index("tensor") * share_count, share_count)
    return lax.all_gather(finished, "tensor", axis=0, tiled=True)


def body(tokens, cotangent, gains, w_gate, w_up, w_down):
    gate_weight = w_gate[0]
    up_weight = w_up[0]
    down_weight = w_down[0]
    column_block = gate_weight.shape[0]
    hidden_block = gate_weight.shape[1]
    leading = lax.axis_index("segment") == 0
    trailing = jnp.logical_not(leading)

    def output_rows(wide):

        def complete(values, first_row, count):
            return (lax.dynamic_slice_in_dim(wide, first_row, count, 0) + values).astype(
                jnp.bfloat16
            )

        return complete

    def gradient_rows(unit, inverse, incoming):

        def complete(values, first_row, count):
            return norm_back(
                lax.dynamic_slice_in_dim(unit, first_row, count, 0),
                lax.dynamic_slice_in_dim(inverse, first_row, count, 0),
                gains,
                values,
                lax.dynamic_slice_in_dim(incoming, first_row, count, 0),
            )

        return complete

    def fold_down(hidden, active):
        initial = jnp.zeros((hidden.shape[0], column_block), jnp.float32)
        piece = lax.all_gather(hidden, "dp", axis=1, tiled=True)

        def compute(current):
            return contract_last(piece, down_weight)

        return lax.cond(active, compute, unchanged, initial)

    def fold_back(d_gate, d_up, active):
        initial = jnp.zeros((d_gate.shape[0], column_block), jnp.float32)
        pieces = (
            lax.all_gather(d_gate, "dp", axis=1, tiled=True),
            lax.all_gather(d_up, "dp", axis=1, tiled=True),
        )

        def compute(current):
            return contract_last(pieces[0], gate_weight) + contract_last(pieces[1], up_weight)

        return lax.cond(active, compute, unchanged, initial)

    def forward_terms(columns):
        return (
            jnp.dot(columns, gate_weight, preferred_element_type=jnp.float32),
            jnp.dot(columns, up_weight, preferred_element_type=jnp.float32),
        )

    def late_grad_terms(columns):
        return (
            jnp.dot(columns, down_weight, preferred_element_type=jnp.float32),
            jnp.zeros((columns.shape[0], hidden_block), jnp.float32),
        )

    def spare_terms(columns):
        empty = jnp.zeros((columns.shape[0], hidden_block), jnp.float32)
        return (empty, empty)

    wide_in, unit_in, inverse_in = normalize(tokens)
    normed_in = (unit_in * gains).astype(jnp.bfloat16)
    entry_cols = to_columns(jnp.where(leading, normed_in, cotangent))
    first_part, second_part = lax.cond(leading, forward_terms, late_grad_terms, entry_cols)
    first_sum, second_sum = hidden_sums(first_part, second_part)
    early_gate = first_sum.astype(jnp.bfloat16)
    early_up = second_sum.astype(jnp.bfloat16)
    early_hidden = (jax.nn.silu(first_sum) * second_sum).astype(jnp.bfloat16)
    early_out = sum_back(fold_down(early_hidden, leading), output_rows(wide_in))
    arrived, held_gate, held_up = from_behind((early_out, early_gate, early_up), "segment", 1)
    wide_mid, unit_mid, inverse_mid = normalize(arrived)
    normed_mid = (unit_mid * gains).astype(jnp.bfloat16)
    mid_cols = to_columns(normed_mid)
    gate_part, up_part = lax.cond(leading, spare_terms, forward_terms, mid_cols)
    late_gate_sum, late_up_sum = hidden_sums(gate_part, up_part)
    late_gate = late_gate_sum.astype(jnp.bfloat16)
    late_up = late_up_sum.astype(jnp.bfloat16)
    late_hidden = (jax.nn.silu(late_gate_sum) * late_up_sum).astype(jnp.bfloat16)
    late_d_gate, late_d_up = input_grads(first_sum, late_gate, late_up)
    late_out = sum_back(fold_down(late_hidden, trailing), output_rows(wide_mid))
    d_mid = sum_back(
        fold_back(late_d_gate, late_d_up, trailing), gradient_rows(unit_mid, inverse_mid, cotangent)
    )
    returned, kept_gate, kept_up = from_behind((d_mid, held_gate, held_up), "segment", -1)
    back_cols = to_columns(returned)

    def early_grad_term(columns):
        return jnp.dot(columns, down_weight, preferred_element_type=jnp.float32)

    def spare_term(columns):
        return jnp.zeros((columns.shape[0], hidden_block), jnp.float32)

    grad_part = lax.cond(leading, early_grad_term, spare_term, back_cols)
    d_hidden_early = lax.psum_scatter(
        grad_part.astype(jnp.bfloat16), "dp", scatter_dimension=1, tiled=True
    ).astype(jnp.float32)
    early_d_gate, early_d_up = input_grads(d_hidden_early, kept_gate, kept_up)
    d_tokens = sum_back(
        fold_back(early_d_gate, early_d_up, leading), gradient_rows(unit_in, inverse_in, returned)
    )
    acts = jnp.where(leading, early_out, late_out)[None]
    grads = jnp.where(leading, d_tokens, d_mid)[None]
    return (acts, grads)


def solution(mesh):
    in_specs = (
        P("dp", None),
        P("dp", None),
        P("segment", None),
        P("segment", "dp", "tensor"),
        P("segment", "dp", "tensor"),
        P("segment", "dp", "tensor"),
    )
    out_specs = (P("segment", "dp", None), P("segment", "dp", None))
    return jax.shard_map(body, mesh=mesh, in_specs=in_specs, out_specs=out_specs, check_vma=False)
```

profile of v0, /device:TPU:0, one launch (start us, length us, event | category | flops | bytes accessed | tf_op | source)
XLA Modules:
  0.0 1663.9 jit_solution(2411397859032944513)
XLA Ops:
  17.6 10.3 all-to-all-done
  27.9 21.7 %conditional.7 = (bf16[256,13824]{1,0:T(8,128)(2,1)}, bf16[256,13824]{1,0:T(8,128)(2,1)}) conditional(s32[]{:T(128)} %convert_element_type.134, (bf16[256,640]{1,0:T(8,128)(2,1)S(1)}, bf16[640,13824]{1,0:T(8,128)(2,1)}) %tuple.134, (bf16[256,640]{1,0:T(8,128)(2,1)S(1)}, bf16[640,13824]{1,0:T(8,128)(2,1)}, bf16[640,13824]{1,0:T(8,128)(2,1)}) %tuple.142), branch_computations={%region_1.2_spmd, %region_2.3_spmd} | conditional | flops 9059696640 | bytes 120979496 | solution.py:149
  27.9 13.9 fusion.27
  49.6 10.3 copy.82
  59.9 10.3 copy.84
  70.3 117.8 %reduce-scatter.28.cloned.1.call-done = bf16[1728,256]{1,0:T(8,128)(2,1)} async-done(((bf16[13824,256]{1,0:T(8,128)(2,1)}), bf16[1728,256]{1,0:T(8,128)(2,1)}) %reduce-scatter.28.cloned.1.call-update) | async-done | bytes 884752
  188.1 132.3 %reduce-scatter.30.cloned.1.call-done = bf16[1728,256]{1,0:T(8,128)(2,1)} async-done(((bf16[13824,256]{1,0:T(8,128)(2,1)}), bf16[1728,256]{1,0:T(8,128)(2,1)}) %reduce-scatter.30.cloned.1.call-update) | async-done | bytes 884752
  323.4 108.0 %all-gather.7.cloned.1.call-done = bf16[256,13824]{0,1:T(8,128)(2,1)} async-done(((bf16[256,1728]{0,1:T(8,128)(2,1)}), bf16[256,13824]{0,1:T(8,128)(2,1)}) %all-gather.7.cloned.1.call-update) | async-done | bytes 7077904 | tf_op jit(solution)/shard_map/all_gather | solution.py:111
  431.4 18.6 %conditional.8 = (bf16[256,640]{1,0:T(8,128)(2,1)S(1)}) conditional(s32[]{:T(128)} %convert_element_type.134, () %tuple.54, (bf16[256,13824]{0,1:T(8,128)(2,1)}, bf16[640,13824]{1,0:T(8,128)(2,1)}) %tuple.135), branch_computations={%region_5.6_spmd, %region_6.7_spmd} | conditional | flops 4529848320 | bytes 25100296 | solution.py:116
  431.8 18.2 %fusion.29 = bf16[256,640]{1,0:T(8,128)(2,1)S(1)} fusion(bf16[256,13824]{0,1:T(8,128)(2,1)} %get-tuple-element.117, bf16[640,13824]{1,0:T(8,128)(2,1)} %get-tuple-element.67), kind=kOutput, calls=%fused_computation.66 | convolution fusion | flops 4529848320 | bytes 25100288 | tf_op jit(solution)/shard_map/cond/branch_1_fun/dot_general | solution.py:22
  450.0 11.6 all_to_all.133
  462.4 10.8 reduce-scatter.20.cloned.1.call-done
  489.9 10.8 all-to-all-done.2
  507.3 10.3 copy.86
  528.0 131.5 %reduce-scatter.32.cloned.1.call-done = bf16[1728,256]{1,0:T(8,128)(2,1)} async-done(((bf16[13824,256]{1,0:T(8,128)(2,1)}), bf16[1728,256]{1,0:T(8,128)(2,1)}) %reduce-scatter.32.cloned.1.call-update) | async-done | bytes 884752
  659.6 131.6 %reduce-scatter.34.cloned.1.call-done = bf16[1728,256]{1,0:T(8,128)(2,1)} async-done(((bf16[13824,256]{1,0:T(8,128)(2,1)}), bf16[1728,256]{1,0:T(8,128)(2,1)}) %reduce-scatter.34.cloned.1.call-update) | async-done | bytes 884752
  796.1 107.2 %all-gather.11.cloned.1.call-done = bf16[256,13824]{0,1:T(8,128)(2,1)} async-done(((bf16[256,1728]{0,1:T(8,128)(2,1)}), bf16[256,13824]{0,1:T(8,128)(2,1)}) %all-gather.11.cloned.1.call-update) | async-done | bytes 7077904 | tf_op jit(solution)/shard_map/all_gather | solution.py:121
  903.2 109.4 %all-gather.13.cloned.1.call-done = bf16[256,13824]{0,1:T(8,128)(2,1)} async-done(((bf16[256,1728]{0,1:T(8,128)(2,1)}), bf16[256,13824]{0,1:T(8,128)(2,1)}) %all-gather.13.cloned.1.call-update) | async-done | bytes 7077904 | tf_op jit(solution)/shard_map/all_gather | solution.py:122
  1012.7 11.7 all_to_all.134
  1025.3 45.8 %reduce-scatter.24.cloned.1.call-done = bf16[16,5120]{1,0:T(8,128)(2,1)} async-done(((bf16[32,5120]{1,0:T(8,128)(2,1)}), bf16[16,5120]{1,0:T(8,128)(2,1)}) %reduce-scatter.24.cloned.1.call-update) | async-done | bytes 163856 | tf_op jit(solution)/shard_map/reduce_scatter | solution.py:71
  1089.7 10.5 all-to-all-done.5
  1100.3 14.0 conditional.12
  1100.5 13.8 fusion.33
  1114.3 10.3 copy.90
  1134.3 117.5 %reduce-scatter.36.cloned.1.call-done = bf16[1728,256]{1,0:T(8,128)(2,1)} async-done(((bf16[13824,256]{1,0:T(8,128)(2,1)}), bf16[1728,256]{1,0:T(8,128)(2,1)}) %reduce-scatter.36.cloned.1.call-update) | async-done | bytes 884752
  1255.9 106.2 %all-gather.9.cloned.1.call-done = bf16[256,13824]{0,1:T(8,128)(2,1)} async-done(((bf16[256,1728]{0,1:T(8,128)(2,1)}), bf16[256,13824]{0,1:T(8,128)(2,1)}) %all-gather.9.cloned.1.call-update) | async-done | bytes 7077904 | tf_op jit(solution)/shard_map/all_gather | solution.py:111
  1376.0 98.8 %all-gather.15.cloned.1.call-done = bf16[256,13824]{0,1:T(8,128)(2,1)} async-done(((bf16[256,1728]{0,1:T(8,128)(2,1)}), bf16[256,13824]{0,1:T(8,128)(2,1)}) %all-gather.15.cloned.1.call-update) | async-done | bytes 7077904 | tf_op jit(solution)/shard_map/all_gather | solution.py:121
  1474.9 109.4 %all-gather.17.cloned.1.call-done = bf16[256,13824]{0,1:T(8,128)(2,1)} async-done(((bf16[256,1728]{0,1:T(8,128)(2,1)}), bf16[256,13824]{0,1:T(8,128)(2,1)}) %all-gather.17.cloned.1.call-update) | async-done | bytes 7077904 | tf_op jit(solution)/shard_map/all_gather | solution.py:122
  1584.3 38.1 %conditional.13 = (bf16[256,640]{1,0:T(8,128)(2,1)}) conditional(s32[]{:T(128)} %convert_element_type.134, () %tuple.64, (bf16[256,13824]{0,1:T(8,128)(2,1)}, bf16[640,13824]{1,0:T(8,128)(2,1)}, bf16[256,13824]{0,1:T(8,128)(2,1)}, bf16[640,13824]{1,0:T(8,128)(2,1)}) %tuple.145), branch_computations={%region_23.24_spmd, %region_24.25_spmd} | conditional | flops 9060024320 | bytes 51183624 | solution.py:128
  1584.6 18.9 %fusion.35 = f32[256,640]{1,0:T(8,128)} fusion(bf16[256,13824]{0,1:T(8,128)(2,1)} %get-tuple-element.125, bf16[640,13824]{1,0:T(8,128)(2,1)} %get-tuple-element.80), kind=kOutput, calls=%fused_computation.72 | convolution fusion | flops 4529848320 | bytes 25427968 | tf_op jit(solution)/shard_map/cond/branch_1_fun/dot_general | solution.py:22
  1603.5 19.0 %convolution_add_fusion.1 = bf16[256,640]{1,0:T(8,128)(2,1)} fusion(f32[256,640]{1,0:T(8,128)} %fusion.35, bf16[256,13824]{0,1:T(8,128)(2,1)} %get-tuple-element.127, bf16[640,13824]{1,0:T(8,128)(2,1)} %get-tuple-element.82), kind=kOutput, calls=%fused_computation.1 | convolution fusion | flops 4530176000 | bytes 25755648 | tf_op jit(solution)/shard_map/cond/branch_1_fun/dot_general | solution.py:22
  1636.0 11.4 reduce-scatter.26.cloned.1.call-done
  (109 shorter events, 138.3 us)
Async XLA Ops:
  10.2 17.7 %all-to-all-start = ((bf16[32,8,640]{2,0,1:T(8,128)(2,1)}), bf16[32,8,640]{2,0,1:T(8,128)(2,1)S(1)}, u32[]{:S(2)}, u32[]{:S(2)}) async-start(bf16[32,8,640]{2,0,1:T(8,128)(2,1)} %bitcast.87), calls=%async_computation | async-start | bytes 655360 | tf_op jit(solution)/shard_map/all_to_all | solution.py:51
  17.5 170.5 %reduce-scatter.28.cloned.1.call-start = ((), (), s32[]{:S(2)}) async-start(), calls=%async_computation.26 | async-start | bytes 7962624
  27.9 13.9 copy-start.7
  59.9 260.4 %reduce-scatter.30.cloned.1.call-start = ((), (), s32[]{:S(2)}) async-start(), calls=%async_computation.27 | async-start | bytes 7962624
  70.2 361.1 %all-gather.7.cloned.1.call-start = ((), (), s32[]{:S(2)}) async-start(), calls=%async_computation.16 | async-start | bytes 7962624 | tf_op jit(solution)/shard_map/all_gather | solution.py:111
  323.3 149.8 %reduce-scatter.20.cloned.1.call-start = ((), (), s32[]{:S(2)}) async-start(), calls=%async_computation.17 | async-start | bytes 491520 | tf_op jit(solution)/shard_map/reduce_scatter | solution.py:71
  431.3 52.0 %copy-start.3 = (f32[1,5120]{1,0:T(1,128)S(1)}, f32[1,5120]{1,0:T(1,128)}, u32[]{:S(2)}) copy-start(f32[1,5120]{1,0:T(1,128)} %param.22) | copy-start | bytes 61444
  480.7 2.5 collective-permute-start
  484.3 16.3 all-to-all-start.2
  489.8 169.7 %reduce-scatter.32.cloned.1.call-start = ((), (), s32[]{:S(2)}) async-start(), calls=%async_computation.28 | async-start | bytes 7962624
  517.6 273.6 %reduce-scatter.34.cloned.1.call-start = ((), (), s32[]{:S(2)}) async-start(), calls=%async_computation.29 | async-start | bytes 7962624
  527.8 263.4 %copy-start = (bf16[1728,256]{1,0:T(8,128)(2,1)S(1)}, bf16[1728,256]{1,0:T(8,128)(2,1)}, u32[]{:S(2)}) copy-start(bf16[1728,256]{1,0:T(8,128)(2,1)} %reduce-scatter.28.cloned.1.call-done) | copy-start | bytes 2654212
  527.8 375.4 %all-gather.11.cloned.1.call-start = ((), (), s32[]{:S(2)}) async-start(), calls=%async_computation.20 | async-start | bytes 7962624 | tf_op jit(solution)/shard_map/all_gather | solution.py:121
  795.2 217.4 %all-gather.13.cloned.1.call-start = ((), (), s32[]{:S(2)}) async-start(), calls=%async_computation.21 | async-start | bytes 7962624 | tf_op jit(solution)/shard_map/all_gather | solution.py:122
  796.0 275.1 %reduce-scatter.24.cloned.1.call-start = ((), (), s32[]{:S(2)}) async-start(), calls=%async_computation.22 | async-start | bytes 491520 | tf_op jit(solution)/shard_map/reduce_scatter | solution.py:71
  1012.7 59.5 %copy-start.4 = (bf16[32,5120]{1,0:T(8,128)(2,1)S(1)}, bf16[32,5120]{1,0:T(8,128)(2,1)}, u32[]{:S(2)}) copy-start(bf16[32,5120]{1,0:T(8,128)(2,1)} %param.21) | copy-start | bytes 983044
  1079.9 3.5 collective-permute-start.1
  1084.2 16.1 all-to-all-start.5
  1089.7 162.2 %reduce-scatter.36.cloned.1.call-start = ((), (), s32[]{:S(2)}) async-start(), calls=%async_computation.30 | async-start | bytes 7962624
  1124.5 237.6 %all-gather.9.cloned.1.call-start = ((), (), s32[]{:S(2)}) async-start(), calls=%async_computation.18 | async-start | bytes 7962624 | tf_op jit(solution)/shard_map/all_gather | solution.py:111
  1125.3 349.6 %all-gather.15.cloned.1.call-start = ((), (), s32[]{:S(2)}) async-start(), calls=%async_computation.23 | async-start | bytes 7962624 | tf_op jit(solution)/shard_map/all_gather | solution.py:121
  1125.3 3.3 collective-permute-start.4
  1126.7 3.3 collective-permute-start.2
  1128.7 4.3 collective-permute-start.5
  1130.0 4.3 collective-permute-start.3
  1255.2 329.1 %all-gather.17.cloned.1.call-start = ((), (), s32[]{:S(2)}) async-start(), calls=%async_computation.24 | async-start | bytes 7962624 | tf_op jit(solution)/shard_map/all_gather | solution.py:122
  1362.2 4.2 copy-start.6
  1362.2 13.7 copy-start.1
  1362.9 12.1 all-to-all-start.3
  1366.4 259.6 %reduce-scatter.22.cloned.1.call-start = ((), (), s32[]{:S(2)}) async-start(), calls=%async_computation.19 | async-start | bytes 491520 | tf_op jit(solution)/shard_map/reduce_scatter | solution.py:71
  1622.5 12.0 all-to-all-start.6
  1625.9 21.5 %reduce-scatter.26.cloned.1.call-start = ((), (), s32[]{:S(2)}) async-start(), calls=%async_computation.25 | async-start | bytes 491520 | tf_op jit(solution)/shard_map/reduce_scatter | solution.py:71
  (2 other events, 4.1 us)
Sparse Core Ops, SparseCore 0:
  60.0 128.0 reduce-scatter.27
  192.2 128.0 reduce-scatter.29
  323.5 107.8 all-gather.6
  462.5 10.5 reduce-scatter.19
  517.7 141.7 reduce-scatter.31
  663.1 128.0 reduce-scatter.33
  795.4 107.8 all-gather.10
  905.7 106.9 all-gather.12
  1025.3 45.7 reduce-scatter.23
  1124.7 127.1 reduce-scatter.35
  1254.3 107.8 all-gather.8
  1364.5 110.3 all-gather.14
  1477.3 106.9 all-gather.16
  1587.1 10.5 reduce-scatter.21
  1635.4 11.9 reduce-scatter.25
where the time goes:
time: 1670 us; the launch traced here: 1660 us
  waiting for transfers between devices  1390 us (83%)
  matrix products  91.5 us (5%)
  local copies, waits for them, and re-layouts  64.1 us (4%)
  blocking collectives  49.2 us (3%)
  starting transfers between devices  33.8 us (2%)
  other arithmetic  20.8 us (1%)
    unnamed x20, waiting for transfers between devices  633 us
    all_gather x2, waiting for transfers between devices, fold_back(): lax.all_gather(d_up, 'dp', axis=1, tiled=True)  219 us
    all_gather x2, waiting for transfers between devices, fold_down(): piece = lax.all_gather(hidden, 'dp', axis=1, tiled=True)  214 us
    all_gather x2, waiting for transfers between devices, fold_back(): lax.all_gather(d_gate, 'dp', axis=1, tiled=True)  206 us
    reduce_scatter x4, waiting for transfers between devices, sum_back(): lax.psum_scatter(rows_part.astype(jnp.bfloat16), 'tensor', scatter_dimens...  68 us
    dot_general x3, matrix products, contract_last(): lax.dot_general(left, right, (((1,), (1,)), ((), ())), preferred_element_...  56.1 us
    unnamed x19, local copies, waits for them, and re-layouts  51.2 us
  transfers between devices with their start and end apart: 26, of which 25 were waited for; matrix products, arithmetic and copies ran while one was open for 4% of the time, Pallas kernels for 0%

commit v1 on v0

v1 whole, which is shorter than its diff:
```python
import jax
import jax.numpy as jnp
from jax import lax
from jax.sharding import PartitionSpec as P

EPSILON = 1e-06
BF16 = jnp.bfloat16
F32 = jnp.float32

GATHER_SHARE = 0.5
SCATTER_SHARE = 0.5
PAIR_FIRST = 2 / 3


def cut(width, share):
    lanes = 128
    whole = width // lanes
    return min(max(int(whole * share + 0.5), 1), whole - 1) * lanes


def contract_last(left, right):
    return lax.dot_general(left, right, (((1,), (1,)), ((), ())), preferred_element_type=F32)


def dot(left, right):
    return jnp.dot(left, right, preferred_element_type=F32)


def swap(value, axis, step=1):
    count = lax.axis_size(axis)
    return lax.ppermute(value, axis, [(i, i ^ step) for i in range(count)])


def line_groups():
    count = lax.axis_size("dp")
    return [list(range(start, count, 2)) for start in range(2)]


def line_exchange(value, axis):
    return lax.all_to_all(
        value, "dp", split_axis=axis, concat_axis=axis, tiled=True, axis_index_groups=line_groups()
    )


def pair_relative(value):
    count = lax.axis_size("dp")
    split = value.reshape((count // 2, 2, value.shape[0] // count) + value.shape[1:])
    own_first = jnp.where(lax.axis_index("dp") % 2 == 0, split, split[:, ::-1])
    return own_first.reshape(value.shape)


def scatter_call(value):
    return lax.psum_scatter(value, "dp", scatter_dimension=0, tiled=True).astype(F32)


def scatter_hops(value):
    count = lax.axis_size("dp")
    rows = value.shape[0] // count
    width = value.shape[1]
    split = value.reshape(count // 2, 2, rows, width)
    edge = cut(width, PAIR_FIRST)
    first, second = split[..., :edge], split[..., edge:]
    first_in = swap(first[:, 1], "dp")
    second_sum = jnp.sum(line_exchange(second, 0).astype(F32), axis=0).astype(BF16)
    first_sum = (first[:, 0].astype(F32) + first_in.astype(F32)).astype(BF16)
    second_in = swap(second_sum[1], "dp")
    first_out = jnp.sum(line_exchange(first_sum, 0).astype(F32), axis=0)
    second_out = second_sum[0].astype(F32) + second_in.astype(F32)
    return jnp.concatenate([first_out, second_out], axis=1)


def gather_call(value):
    return lax.all_gather(value, "dp", axis=0, tiled=True)


def gather_hops(value):
    count = lax.axis_size("dp")
    rows, width = value.shape
    edge = cut(width, PAIR_FIRST)

    def spread(part):
        return line_exchange(jnp.broadcast_to(part[None], (count // 2,) + part.shape), 0)

    first, second = value[:, :edge], value[:, edge:]
    second_pair = jnp.stack([second, swap(second, "dp")])
    first_line = spread(first)
    second_all = spread(second_pair)
    first_all = jnp.stack([first_line, swap(first_line, "dp")], axis=1)
    return (
        first_all.reshape(count * rows, edge),
        second_all.reshape(count * rows, width - edge),
    )


def sum_shares(partial_value):
    total = partial_value.astype(BF16)
    total = (total.astype(F32) + swap(total, "segment").astype(F32)).astype(BF16)
    step = 1
    while step < lax.axis_size("tensor"):
        wide = total.astype(F32) + swap(total, "tensor", step).astype(F32)
        step *= 2
        total = wide.astype(BF16) if step < lax.axis_size("tensor") else wide
    return total.astype(F32)


def input_grads(d_hidden, stash_gate, stash_up):
    gate_pre = stash_gate.astype(F32)
    up_pre = stash_up.astype(F32)
    sigmoid_gate = jax.nn.sigmoid(gate_pre)
    d_gate = (d_hidden * up_pre * sigmoid_gate * (1.0 + gate_pre * (1.0 - sigmoid_gate))).astype(BF16)
    d_up = (d_hidden * gate_pre * sigmoid_gate).astype(BF16)
    return (d_gate, d_up)


def body(tokens, cotangent, gains, w_gate, w_up, w_down):
    gate_weight, up_weight, down_weight = w_gate[0], w_up[0], w_down[0]
    column_block, held = gate_weight.shape
    half = held // 2
    rows, features = tokens.shape
    segment = lax.axis_index("segment")
    block = lax.axis_index("dp")
    leading = segment == 0

    def other_half(weight):
        given = lax.dynamic_slice_in_dim(weight, (1 - segment) * half, half, 1)
        return swap(given, "segment")

    gate_other, up_other, down_other = (
        other_half(gate_weight),
        other_half(up_weight),
        other_half(down_weight),
    )

    def early(function, own, other, value):
        return lax.cond(
            leading,
            lambda v, mine, theirs: function(v, mine[:, :half]),
            lambda v, mine, theirs: function(v, theirs),
            value,
            own,
            other,
        )

    def late(function, own, other, value):
        return lax.cond(
            leading,
            lambda v, mine, theirs: function(v, theirs),
            lambda v, mine, theirs: function(v, mine[:, half:]),
            value,
            own,
            other,
        )

    def product(value, weight):
        return dot(value, weight).astype(BF16)

    def own_rows(value):
        return lax.dynamic_slice_in_dim(value, block * rows, rows, 0)

    def to_rows(value):
        return lax.all_to_all(value, "dp", split_axis=0, concat_axis=1, tiled=True)

    mixed = lax.all_to_all(
        jnp.where(leading, tokens, cotangent), "dp", split_axis=1, concat_axis=0, tiled=True
    )
    mixed_other = swap(mixed, "segment")
    token_cols = jnp.where(leading, mixed, mixed_other)
    cotangent_cols = jnp.where(leading, mixed_other, mixed)
    gain_own = lax.dynamic_slice_in_dim(gains, block * column_block, column_block, 1)
    gain_other = swap(gain_own, "segment")
    early_gain = jnp.where(leading, gain_own, gain_other)
    late_gain = jnp.where(leading, gain_other, gain_own)

    wide_tokens = tokens.astype(F32)
    inverse_in = lax.rsqrt(jnp.mean(wide_tokens * wide_tokens, axis=1, keepdims=True) + EPSILON)

    def hidden_inputs(apply, cols, gain_row, inverse):
        scaled = (cols.astype(F32) * gain_row).astype(BF16)
        gate_part = apply(product, gate_weight, gate_other, scaled)
        up_part = apply(product, up_weight, up_other, pair_relative(scaled))
        return scatter_call(gate_part), scatter_hops(up_part)

    def down_product(apply, hidden):
        edge = cut(half, GATHER_SHARE)
        called = gather_call(hidden[:, :edge])
        hop_a, hop_b = gather_hops(hidden[:, edge:])
        mid = edge + hop_a.shape[1]

        def natural(v, w):
            return contract_last(v, w[:, :edge])

        def relative(v, w):
            return contract_last(v[0], w[:, edge:mid]) + contract_last(v[1], w[:, mid:])

        return apply(natural, down_weight, down_other, called) + pair_relative(
            apply(relative, down_weight, down_other, (hop_a, hop_b))
        )

    def normed_grads(apply, d_gate, d_up):
        called = gather_call(d_gate)
        hop_a, hop_b = gather_hops(d_up)
        edge = hop_a.shape[1]

        def relative(v, w):
            return contract_last(v[0], w[:, :edge]) + contract_last(v[1], w[:, edge:])

        return apply(contract_last, gate_weight, gate_other, called) + pair_relative(
            apply(relative, up_weight, up_other, (hop_a, hop_b))
        )

    def projection(d_gate, d_up, gate, up):
        mine = jnp.sum(d_gate.astype(F32) * gate + d_up.astype(F32) * up, axis=1)
        everyone = lax.all_gather(mine, ("segment", "dp", "tensor"))
        shape = (lax.axis_size("segment"), lax.axis_size("dp"), lax.axis_size("tensor"), rows)
        return jnp.sum(everyone.reshape(shape), axis=(0, 2)).reshape(-1, 1) / features

    def norm_back(cols, inverse, gain_row, d_normed, mean_value, incoming):
        unit = cols.astype(F32) * inverse
        weighted = d_normed * gain_row
        return (incoming.astype(F32) + inverse * (weighted - unit * mean_value)).astype(BF16)

    gate_sum, up_sum = hidden_inputs(early, token_cols, early_gain, inverse_in)
    early_gate, early_up = gate_sum * inverse_in, up_sum * inverse_in
    stash_gate, stash_up = early_gate.astype(BF16), early_up.astype(BF16)
    early_hidden = (jax.nn.silu(early_gate) * early_up).astype(BF16)
    late_d_hidden = scatter_call(late(product, down_weight, down_other, cotangent_cols))
    inverse_all = lax.all_gather(inverse_in, "dp", axis=0, tiled=True)
    early_out = (
        token_cols.astype(F32) + sum_shares(down_product(early, early_hidden))
    ).astype(BF16)

    wide_mid = early_out.astype(F32)
    squares = lax.all_gather(jnp.sum(wide_mid * wide_mid, axis=1), "dp")
    inverse_mid = lax.rsqrt(jnp.sum(squares, axis=0)[:, None] / features + EPSILON)
    gate_sum, up_sum = hidden_inputs(late, early_out, late_gain, inverse_mid)
    inverse_own = own_rows(inverse_mid)
    late_gate, late_up = gate_sum * inverse_own, up_sum * inverse_own
    late_hidden = (jax.nn.silu(late_gate) * late_up).astype(BF16)
    d_gate, d_up = input_grads(late_d_hidden, late_gate.astype(BF16), late_up.astype(BF16))
    mean_value = projection(d_gate, d_up, late_gate, late_up)
    d_normed = sum_shares(normed_grads(late, d_gate, d_up))
    d_early = norm_back(early_out, inverse_mid, late_gain, d_normed, mean_value, cotangent_cols)
    late_out = (wide_mid + sum_shares(down_product(late, late_hidden))).astype(BF16)
    acts = to_rows(jnp.where(leading, early_out, late_out))[None]

    edge = cut(half, SCATTER_SHARE)
    d_hidden = jnp.concatenate(
        [
            scatter_call(early(lambda v, w: product(v, w[:, :edge]), down_weight, down_other, d_early)),
            scatter_hops(
                early(
                    lambda v, w: product(v, w[:, edge:]),
                    down_weight,
                    down_other,
                    pair_relative(d_early),
                )
            ),
        ],
        axis=1,
    )
    d_gate, d_up = input_grads(d_hidden, stash_gate, stash_up)
    mean_value = projection(d_gate, d_up, early_gate, early_up)
    d_normed = sum_shares(normed_grads(early, d_gate, d_up))
    d_tokens = norm_back(token_cols, inverse_all, early_gain, d_normed, mean_value, d_early)
    grads = to_rows(jnp.where(leading, d_tokens, d_early))[None]
    return (acts, grads)


def solution(mesh):
    in_specs = (
        P("dp", None),
        P("dp", None),
        P("segment", None),
        P("segment", "dp", "tensor"),
        P("segment", "dp", "tensor"),
        P("segment", "dp", "tensor"),
    )
    out_specs = (P("segment", "dp", None), P("segment", "dp", None))
    return jax.shard_map(body, mesh=mesh, in_specs=in_specs, out_specs=out_specs, check_vma=False)
```

time: 1670 us -> 969 us (0.58)
  waiting for transfers between devices: 1390 us -> 489 us
  blocking collectives: 49.2 us -> 159 us
  starting transfers between devices: 33.8 us -> 96.6 us
  other arithmetic: 20.8 us -> 37.5 us
    all_gather x6 -> x4, waiting for transfers between devices: 639 us -> 0.08 us  [gather_call(): return lax.all_gather(value, 'dp', axis=0, tiled=True)]
    unnamed x20 -> x8, waiting for transfers between devices: 633 us -> 0.14 us
    all_to_all x5 -> x16, waiting for transfers between devices: 41.7 us -> 276 us  [the longest x14 267 us: line_exchange(): lax.all_to_all(value, 'dp', split_axis=axis, concat_axis=axis, tiled=True...]
    ppermute x6 -> x27, waiting for transfers between devices: 7.15 us -> 165 us  [swap(): return lax.ppermute(value, axis, [(i, i ^ step) for i in range(count)])]
    unnamed x0 -> x3, blocking collectives: none -> 99.5 us
    unnamed x19 -> x32, local copies, waits for them, and re-layouts: 51.2 us -> 2.67 us
    all_to_all x5 -> x16, starting transfers between devices: 25.2 us -> 63.2 us  [the longest x14 53.9 us: line_exchange(): lax.all_to_all(value, 'dp', split_axis=axis, concat_axis=axis, tiled=True...]
    ppermute x6 -> x27, starting transfers between devices: 7.83 us -> 33.1 us  [swap(): return lax.ppermute(value, axis, [(i, i ^ step) for i in range(count)])]
  transfers between devices with their start and end apart: 26 -> 51, of which waited for: 25 -> 32; matrix products, arithmetic and copies ran while one was open for 4% -> 17% of each run, Pallas kernels for 0% -> 0%
where the time goes in v1:
time: 969 us; the launch traced here: 957 us
  waiting for transfers between devices  489 us (50%)
  blocking collectives  159 us (16%)
  matrix products  104 us (11%)
  starting transfers between devices  96.6 us (10%)
  local copies, waits for them, and re-layouts  54.7 us (6%)
  other arithmetic  37.5 us (4%)
  between operations  15.9 us (2%)
    all_to_all x14, waiting for transfers between devices, line_exchange(): lax.all_to_all(value, 'dp', split_axis=axis, concat_axis=axis, tiled=True...  267 us
    ppermute x27, waiting for transfers between devices, swap(): return lax.ppermute(value, axis, [(i, i ^ step) for i in range(count)])  165 us
    unnamed x3, blocking collectives  99.5 us
    all_to_all x14, starting transfers between devices, line_exchange(): lax.all_to_all(value, 'dp', split_axis=axis, concat_axis=axis, tiled=True...  53.9 us
    dot_general x12, matrix products, contract_last(): lax.dot_general(left, right, (((1,), (1,)), ((), ())), preferred_element_...  52.6 us
    dot_general x7, matrix products, dot(): return jnp.dot(left, right, preferred_element_type=F32)  51.1 us
    reduce_scatter x4, waiting for transfers between devices, scatter_call(): lax.psum_scatter(value, 'dp', scatter_dimension=0, tiled=True).astype(F32)  48.2 us
    all_gather x1, blocking collectives, body(): squares = lax.all_gather(jnp.sum(wide_mid * wide_mid, axis=1), 'dp')  41.2 us
  transfers between devices with their start and end apart: 51, of which 32 were waited for; matrix products, arithmetic and copies ran while one was open for 17% of the time, Pallas kernels for 0%

profile of v1, /device:TPU:0, one launch (start us, length us, event | category | flops | bytes accessed | tf_op | source)
XLA Modules:
  0.0 957.3 jit_solution(6877170064653312180)
XLA Ops:
  23.0 18.2 %all_to_all.121 = bf16[32,8,640]{2,0,1:T(8,128)(2,1)S(1)} all-to-all(bf16[32,8,640]{2,0,1:T(8,128)(2,1)S(1)} %bitcast.225), channel_id=1, replica_groups=mesh['segment'=2,'dp'=8,'tensor'=2] {'dp'}, dimensions={1} | all-to-all | bytes 655360 | tf_op jit(solution)/shard_map/all_to_all | solution.py:163
  80.0 18.3 %collective-permute-done.5 = bf16[4,32,4608]{2,1,0:T(8,128)(2,1)S(1)} collective-permute-done((bf16[4,32,4608]{2,1,0:T(8,128)(2,1)}, bf16[4,32,4608]{2,1,0:T(8,128)(2,1)S(1)}, u32[]{:S(2)}, u32[]{:S(2)}) %collective-permute-start.5) | collective-permute-done | bytes 1179680 | tf_op jit(solution)/shard_map/ppermute | solution.py:31
  100.8 18.0 %all-to-all-done.2 = bf16[4,2,32,2304]{3,2,1,0:T(8,128)(2,1)S(1)} async-done(((bf16[4,2,32,2304]{3,2,1,0:T(8,128)(2,1)}), bf16[4,2,32,2304]{3,2,1,0:T(8,128)(2,1)S(1)}, u32[]{:S(2)}, u32[]{:S(2)}) %all-to-all-start.2) | async-done | bytes 1179680 | tf_op jit(solution)/shard_map/all_to_all | solution.py:40
  129.9 35.7 %all-to-all-done.1 = bf16[4,32,4608]{2,1,0:T(8,128)(2,1)S(1)} async-done(((bf16[4,32,4608]{2,1,0:T(8,128)(2,1)}), bf16[4,32,4608]{2,1,0:T(8,128)(2,1)S(1)}, u32[]{:S(2)}, u32[]{:S(2)}) %all-to-all-start.1) | async-done | bytes 1179680 | tf_op jit(solution)/shard_map/all_to_all | solution.py:40
  169.6 8.5 conditional.51
  169.6 8.5 fusion.118
  183.7 20.5 %all-to-all-done.3 = bf16[4,32,2304]{2,1,0:T(8,128)(2,1)S(1)} async-done(((bf16[4,32,2304]{2,1,0:T(8,128)(2,1)}), bf16[4,32,2304]{2,1,0:T(8,128)(2,1)S(1)}, u32[]{:S(2)}, u32[]{:S(2)}) %all-to-all-start.3) | async-done | bytes 589856 | tf_op jit(solution)/shard_map/all_to_all | solution.py:40
  210.3 9.7 %collective-permute-done.7 = bf16[4,32,2304]{2,1,0:T(8,128)(2,1)S(1)} collective-permute-done((bf16[4,32,2304]{2,1,0:T(8,128)(2,1)S(1)}, bf16[4,32,2304]{2,1,0:T(8,128)(2,1)S(1)}, u32[]{:S(2)}, u32[]{:S(2)}) %collective-permute-start.7) | collective-permute-done | bytes 589856 | tf_op jit(solution)/shard_map/ppermute | solution.py:31
  252.0 8.6 conditional.47
  278.0 30.7 %collective-permute-done.11 = bf16[4,32,4608]{2,1,0:T(8,128)(2,1)S(1)} collective-permute-done((bf16[4,32,4608]{2,1,0:T(8,128)(2,1)}, bf16[4,32,4608]{2,1,0:T(8,128)(2,1)S(1)}, u32[]{:S(2)}, u32[]{:S(2)}) %collective-permute-start.11) | collective-permute-done | bytes 1179680 | tf_op jit(solution)/shard_map/ppermute | solution.py:31
  311.2 8.7 all-to-all-done.6
  323.5 41.2 %all-gather.4 = f32[8,1,256]{2,1,0:T(1,128)S(1)} all-gather(f32[1,1,256]{2,1,0:T(1,128)S(1)} %bitcast.246), channel_id=2, replica_groups=mesh['segment'=2,'dp'=8,'tensor'=2] {'dp'}, dimensions={0}, use_global_device_ids=true | all-gather | bytes 9216 | tf_op jit(solution)/shard_map/all_gather | solution.py:233
  366.6 12.9 %collective-permute-start.12 = (bf16[32,2304]{1,0:T(8,128)(2,1)S(1)}, bf16[32,2304]{1,0:T(8,128)(2,1)S(1)}, u32[]{:S(2)}, u32[]{:S(2)}) collective-permute-start(bf16[32,2304]{1,0:T(8,128)(2,1)S(1)} %slice_bitcast_fusion.6), channel_id=1, source_target_pairs={{0,2},{2,0},{4,6},{6,4},{8,10},{10,8},{12,14},{14,12},{1,3},{3,1},... | collective-permute-start | bytes 442376 | tf_op jit(solution)/shard_map/ppermute | solution.py:31
  384.1 33.4 %reduce-scatter.7.cloned.1.call-done = bf16[32,6912]{1,0:T(8,128)(2,1)} async-done(((bf16[256,6912]{1,0:T(8,128)(2,1)}), bf16[32,6912]{1,0:T(8,128)(2,1)}) %reduce-scatter.7.cloned.1.call-update) | async-done | bytes 442384 | tf_op jit(solution)/shard_map/reduce_scatter | solution.py:53
  427.4 40.4 %all-to-all-done.10 = bf16[4,32,4608]{2,1,0:T(8,128)(2,1)S(1)} async-done(((bf16[4,32,4608]{2,1,0:T(8,128)(2,1)}), bf16[4,32,4608]{2,1,0:T(8,128)(2,1)S(1)}, u32[]{:S(2)}, u32[]{:S(2)}) %all-to-all-start.10) | async-done | bytes 1179680 | tf_op jit(solution)/shard_map/all_to_all | solution.py:40
  474.6 39.1 %collective-permute-done.17 = bf16[4,32,4608]{2,1,0:T(8,128)(2,1)} collective-permute-done((bf16[4,32,4608]{2,1,0:T(8,128)(2,1)S(1)}, bf16[4,32,4608]{2,1,0:T(8,128)(2,1)}, u32[]{:S(2)}, u32[]{:S(2)}) %collective-permute-start.17) | collective-permute-done | bytes 1179680 | tf_op jit(solution)/shard_map/ppermute | solution.py:31
  516.6 10.6 %all-to-all-done.11 = bf16[4,2,32,2304]{3,2,1,0:T(8,128)(2,1)} async-done(((bf16[4,2,32,2304]{3,2,1,0:T(8,128)(2,1)}), bf16[4,2,32,2304]{3,2,1,0:T(8,128)(2,1)}, u32[]{:S(2)}, u32[]{:S(2)}) %all-to-all-start.11) | async-done | bytes 1179680 | tf_op jit(solution)/shard_map/all_to_all | solution.py:40
  527.2 8.9 conditional.53
  547.3 40.9 %all-reduce = f32[1024]{0:T(1024)S(1)} all-reduce(f32[1024]{0:T(1024)S(1)} %dynamic-update-slice), channel_id=3, replica_groups=mesh['segment'=2,'dp'=8,'tensor'=2] {'segment','dp','tensor'}, use_global_device_ids=true, to_apply=%add | all-reduce | flops 1024 | bytes 8192
  610.8 10.1 %collective-permute-done.21 = bf16[4,32,2304]{2,1,0:T(8,128)(2,1)S(1)} collective-permute-done((bf16[4,32,2304]{2,1,0:T(8,128)(2,1)}, bf16[4,32,2304]{2,1,0:T(8,128)(2,1)S(1)}, u32[]{:S(2)}, u32[]{:S(2)}) %collective-permute-start.21) | collective-permute-done | bytes 589856 | tf_op jit(solution)/shard_map/ppermute | solution.py:31
  622.9 12.2 %all-to-all-done.13 = bf16[4,2,32,1152]{3,2,1,0:T(8,128)(2,1)S(1)} async-done(((bf16[4,2,32,1152]{3,2,1,0:T(8,128)(2,1)}), bf16[4,2,32,1152]{3,2,1,0:T(8,128)(2,1)S(1)}, u32[]{:S(2)}, u32[]{:S(2)}) %all-to-all-start.13) | async-done | bytes 589856 | tf_op jit(solution)/shard_map/all_to_all | solution.py:40
  643.8 9.9 %all-to-all-done.12 = bf16[4,32,2304]{2,1,0:T(8,128)(2,1)S(1)} async-done(((bf16[4,32,2304]{2,1,0:T(8,128)(2,1)}), bf16[4,32,2304]{2,1,0:T(8,128)(2,1)S(1)}, u32[]{:S(2)}, u32[]{:S(2)}) %all-to-all-start.12) | async-done | bytes 589856 | tf_op jit(solution)/shard_map/all_to_all | solution.py:40
  653.8 14.8 %reduce-scatter.11.cloned.1.call-done = bf16[32,3456]{1,0:T(8,128)(2,1)} async-done(((bf16[256,3456]{1,0:T(8,128)(2,1)}), bf16[32,3456]{1,0:T(8,128)(2,1)}) %reduce-scatter.11.cloned.1.call-update) | async-done | bytes 221200 | tf_op jit(solution)/shard_map/reduce_scatter | solution.py:53
  676.6 22.0 %all-to-all-done.7 = bf16[4,32,2304]{2,1,0:T(8,128)(2,1)S(1)} async-done(((bf16[4,32,2304]{2,1,0:T(8,128)(2,1)}), bf16[4,32,2304]{2,1,0:T(8,128)(2,1)S(1)}, u32[]{:S(2)}, u32[]{:S(2)}) %all-to-all-start.7) | async-done | bytes 589856 | tf_op jit(solution)/shard_map/all_to_all | solution.py:40
  709.3 35.2 %all-to-all-done.14 = bf16[4,32,4608]{2,1,0:T(8,128)(2,1)S(1)} async-done(((bf16[4,32,4608]{2,1,0:T(8,128)(2,1)}), bf16[4,32,4608]{2,1,0:T(8,128)(2,1)S(1)}, u32[]{:S(2)}, u32[]{:S(2)}) %all-to-all-start.14) | async-done | bytes 1179680 | tf_op jit(solution)/shard_map/all_to_all | solution.py:40
  758.6 20.0 %all-to-all-done.8 = bf16[4,2,32,1152]{3,2,1,0:T(8,128)(2,1)S(1)} async-done(((bf16[4,2,32,1152]{3,2,1,0:T(8,128)(2,1)}), bf16[4,2,32,1152]{3,2,1,0:T(8,128)(2,1)S(1)}, u32[]{:S(2)}, u32[]{:S(2)}) %all-to-all-start.8) | async-done | bytes 589856 | tf_op jit(solution)/shard_map/all_to_all | solution.py:40
  798.0 11.3 %collective-permute-done.23 = bf16[4,32,4608]{2,1,0:T(8,128)(2,1)} collective-permute-done((bf16[4,32,4608]{2,1,0:T(8,128)(2,1)S(1)}, bf16[4,32,4608]{2,1,0:T(8,128)(2,1)}, u32[]{:S(2)}, u32[]{:S(2)}) %collective-permute-start.23) | collective-permute-done | bytes 1179680 | tf_op jit(solution)/shard_map/ppermute | solution.py:31
  812.2 26.9 %all-to-all-done.15 = bf16[4,2,32,2304]{3,2,1,0:T(8,128)(2,1)} async-done(((bf16[4,2,32,2304]{3,2,1,0:T(8,128)(2,1)}), bf16[4,2,32,2304]{3,2,1,0:T(8,128)(2,1)}, u32[]{:S(2)}, u32[]{:S(2)}) %all-to-all-start.15) | async-done | bytes 1179680 | tf_op jit(solution)/shard_map/all_to_all | solution.py:40
  839.0 8.7 conditional.57
  873.5 21.8 %all-reduce.1 = f32[256]{0:T(256)S(1)} all-reduce(f32[256]{0:T(256)S(1)} %get-tuple-element.306), channel_id=4, replica_groups=mesh['segment'=2,'dp'=8,'tensor'=2] {'dp'}, use_global_device_ids=true, to_apply=%add.1 | all-reduce | flops 256 | bytes 2048
  895.5 36.9 %all-reduce.2 = f32[1024]{0:T(1024)S(1)} all-reduce(f32[1024]{0:T(1024)S(1)} %dynamic-update-slice.2), channel_id=5, replica_groups=mesh['segment'=2,'dp'=8,'tensor'=2] {'segment','dp','tensor'}, use_global_device_ids=true, to_apply=%add.2 | all-reduce | flops 1024 | bytes 8192
  940.6 8.5 all-to-all-done.16
  (258 shorter events, 396.2 us)
Async XLA Ops:
  7.2 158.6 %reduce-scatter.5.cloned.1.call-start = ((), (), s32[]{:S(2)}) async-start(), calls=%async_computation.21 | async-start | bytes 3981312 | tf_op jit(solution)/shard_map/reduce_scatter | solution.py:53
  14.7 30.0 %collective-permute-start.3 = (bf16[640,6912]{1,0:T(8,128)(2,1)}, bf16[640,6912]{1,0:T(8,128)(2,1)}, u32[]{:S(2)}, u32[]{:S(2)}) collective-permute-start(bf16[640,6912]{1,0:T(8,128)(2,1)} %dynamic-slice_bitcast_fusion.1), channel_id=1, source_target_pairs={{0,16},{16,0},{1,17},{17,1},{2,18},{18,2},{3,19},{19,3},{4,20},{20... | collective-permute-start | bytes 26542088 | tf_op jit(solution)/shard_map/ppermute | solution.py:31
  22.8 30.3 %collective-permute-start.4 = (bf16[640,6912]{1,0:T(8,128)(2,1)}, bf16[640,6912]{1,0:T(8,128)(2,1)}, u32[]{:S(2)}, u32[]{:S(2)}) collective-permute-start(bf16[640,6912]{1,0:T(8,128)(2,1)} %dynamic-slice_bitcast_fusion), channel_id=1, source_target_pairs={{0,16},{16,0},{1,17},{17,1},{2,18},{18,2},{3,19},{19,3},{4,20},{20... | collective-permute-start | bytes 26542088 | tf_op jit(solution)/shard_map/ppermute | solution.py:31
  63.8 34.5 %collective-permute-start.5 = (bf16[4,32,4608]{2,1,0:T(8,128)(2,1)}, bf16[4,32,4608]{2,1,0:T(8,128)(2,1)S(1)}, u32[]{:S(2)}, u32[]{:S(2)}) collective-permute-start(bf16[4,32,4608]{2,1,0:T(8,128)(2,1)} %slice_bitcast_fusion.2), channel_id=1, source_target_pairs={{0,2},{2,0},{4,6},{6,4},{8,10},{10,8},{12,14},{14,12},{1,3},{3,1},... | collective-permute-start | bytes 3538952 | tf_op jit(solution)/shard_map/ppermute | solution.py:31
  72.8 96.8 %collective-permute-start.1 = (bf16[640,6912]{1,0:T(8,128)(2,1)}, bf16[640,6912]{1,0:T(8,128)(2,1)}, u32[]{:S(2)}, u32[]{:S(2)}) collective-permute-start(bf16[640,6912]{1,0:T(8,128)(2,1)} %dynamic-slice_bitcast_fusion.2), channel_id=1, source_target_pairs={{0,16},{16,0},{1,17},{17,1},{2,18},{18,2},{3,19},{19,3},{4,20},{20... | collective-permute-start | bytes 26542088 | tf_op jit(solution)/shard_map/ppermute | solution.py:31
  75.2 43.7 %all-to-all-start.2 = ((bf16[4,2,32,2304]{3,2,1,0:T(8,128)(2,1)}), bf16[4,2,32,2304]{3,2,1,0:T(8,128)(2,1)S(1)}, u32[]{:S(2)}, u32[]{:S(2)}) async-start(bf16[4,2,32,2304]{3,2,1,0:T(8,128)(2,1)} %slice.230), calls=%async_computation.3 | async-start | bytes 2359296 | tf_op jit(solution)/shard_map/all_to_all | solution.py:40
  118.9 46.7 %all-to-all-start.1 = ((bf16[4,32,4608]{2,1,0:T(8,128)(2,1)}), bf16[4,32,4608]{2,1,0:T(8,128)(2,1)S(1)}, u32[]{:S(2)}, u32[]{:S(2)}) async-start(bf16[4,32,4608]{2,1,0:T(8,128)(2,1)} %fusion.63), calls=%async_computation.2 | async-start | bytes 2359296 | tf_op jit(solution)/shard_map/all_to_all | solution.py:40
  122.4 112.8 %all-gather.10.cloned.1.call-start = ((), (), s32[]{:S(2)}) async-start(), calls=%async_computation.22 | async-start | bytes 1990656 | tf_op jit(solution)/shard_map/all_gather | solution.py:73
  167.8 216.3 %reduce-scatter.9.cloned.1.call-start = ((), (), s32[]{:S(2)}) async-start(), calls=%async_computation.25 | async-start | bytes 3981312 | tf_op jit(solution)/shard_map/reduce_scatter | solution.py:53
  210.3 207.2 %reduce-scatter.7.cloned.1.call-start = ((), (), s32[]{:S(2)}) async-start(), calls=%async_computation.23 | async-start | bytes 3981312 | tf_op jit(solution)/shard_map/reduce_scatter | solution.py:53
  271.0 37.7 %collective-permute-start.11 = (bf16[4,32,4608]{2,1,0:T(8,128)(2,1)}, bf16[4,32,4608]{2,1,0:T(8,128)(2,1)S(1)}, u32[]{:S(2)}, u32[]{:S(2)}) collective-permute-start(bf16[4,32,4608]{2,1,0:T(8,128)(2,1)} %slice_bitcast_fusion), channel_id=1, source_target_pairs={{0,2},{2,0},{4,6},{6,4},{8,10},{10,8},{12,14},{14,12},{1,3},{3,1},... | collective-permute-start | bytes 3538952 | tf_op jit(solution)/shard_map/ppermute | solution.py:31
  274.5 45.5 %all-to-all-start.6 = ((bf16[4,2,32,2304]{3,2,1,0:T(8,128)(2,1)}), bf16[4,2,32,2304]{3,2,1,0:T(8,128)(2,1)S(1)}, u32[]{:S(2)}, u32[]{:S(2)}) async-start(bf16[4,2,32,2304]{3,2,1,0:T(8,128)(2,1)} %slice.238), calls=%async_computation.8 | async-start | bytes 2359296 | tf_op jit(solution)/shard_map/all_to_all | solution.py:40
  319.9 64.0 %all-to-all-start.5 = ((bf16[4,32,4608]{2,1,0:T(8,128)(2,1)}), bf16[4,32,4608]{2,1,0:T(8,128)(2,1)S(1)}, u32[]{:S(2)}, u32[]{:S(2)}) async-start(bf16[4,32,4608]{2,1,0:T(8,128)(2,1)} %fusion.62), calls=%async_computation.7 | async-start | bytes 2359296 | tf_op jit(solution)/shard_map/all_to_all | solution.py:40
  323.5 212.8 %all-gather.14.cloned.1.call-start = ((), (), s32[]{:S(2)}) async-start(), calls=%async_computation.26 | async-start | bytes 3981312 | tf_op jit(solution)/shard_map/all_gather | solution.py:73
  421.5 46.3 %all-to-all-start.10 = ((bf16[4,32,4608]{2,1,0:T(8,128)(2,1)}), bf16[4,32,4608]{2,1,0:T(8,128)(2,1)S(1)}, u32[]{:S(2)}, u32[]{:S(2)}) async-start(bf16[4,32,4608]{2,1,0:T(8,128)(2,1)} %broadcast_in_dim.25), calls=%async_computation.13 | async-start | bytes 2359296 | tf_op jit(solution)/shard_map/all_to_all | solution.py:40
  425.9 43.2 %collective-permute-start.18 = (bf16[32,2304]{1,0:T(8,128)(2,1)S(1)}, bf16[32,2304]{1,0:T(8,128)(2,1)S(1)}, u32[]{:S(2)}, u32[]{:S(2)}) collective-permute-start(bf16[32,2304]{1,0:T(8,128)(2,1)S(1)} %get-tuple-element.301), channel_id=1, source_target_pairs={{0,2},{2,0},{4,6},{6,4},{8,10},{10,8},{12,14},{14,12},{1,3},{3,1},... | collective-permute-start | bytes 442376 | tf_op jit(solution)/shard_map/ppermute | solution.py:31
  467.7 46.0 %collective-permute-start.17 = (bf16[4,32,4608]{2,1,0:T(8,128)(2,1)S(1)}, bf16[4,32,4608]{2,1,0:T(8,128)(2,1)}, u32[]{:S(2)}, u32[]{:S(2)}) collective-permute-start(bf16[4,32,4608]{2,1,0:T(8,128)(2,1)S(1)} %all-to-all-done.10), channel_id=1, source_target_pairs={{0,2},{2,0},{4,6},{6,4},{8,10},{10,8},{12,14},{14,12},{1,3},{3,1},... | collective-permute-start | bytes 3538952 | tf_op jit(solution)/shard_map/ppermute | solution.py:31
  470.3 56.9 %all-to-all-start.11 = ((bf16[4,2,32,2304]{3,2,1,0:T(8,128)(2,1)}), bf16[4,2,32,2304]{3,2,1,0:T(8,128)(2,1)}, u32[]{:S(2)}, u32[]{:S(2)}) async-start(bf16[4,2,32,2304]{3,2,1,0:T(8,128)(2,1)} %broadcast_in_dim.26), calls=%async_computation.14 | async-start | bytes 2359296 | tf_op jit(solution)/shard_map/all_to_all | solution.py:40
  474.6 194.0 %reduce-scatter.11.cloned.1.call-start = ((), (), s32[]{:S(2)}) async-start(), calls=%async_computation.27 | async-start | bytes 1990656 | tf_op jit(solution)/shard_map/reduce_scatter | solution.py:53
  545.7 42.8 %collective-permute-start.20 = (bf16[256,640]{1,0:T(8,128)(2,1)S(1)}, bf16[256,640]{1,0:T(8,128)(2,1)S(1)}, u32[]{:S(2)}, u32[]{:S(2)}) collective-permute-start(bf16[256,640]{1,0:T(8,128)(2,1)S(1)} %add_convert_fusion.1), channel_id=1, source_target_pairs={{0,1},{1,0},{2,3},{3,2},{4,5},{5,4},{6,7},{7,6},{8,9},{9,8},{10,11... | collective-permute-start | bytes 983048 | tf_op jit(solution)/shard_map/ppermute | solution.py:31
  595.0 196.2 %all-gather.12.cloned.1.call-start = ((), (), s32[]{:S(2)}) async-start(), calls=%async_computation.24 | async-start | bytes 1990656 | tf_op jit(solution)/shard_map/all_gather | solution.py:73
  607.1 27.9 %all-to-all-start.13 = ((bf16[4,2,32,1152]{3,2,1,0:T(8,128)(2,1)}), bf16[4,2,32,1152]{3,2,1,0:T(8,128)(2,1)S(1)}, u32[]{:S(2)}, u32[]{:S(2)}) async-start(bf16[4,2,32,1152]{3,2,1,0:T(8,128)(2,1)} %slice.248), calls=%async_computation.17 | async-start | bytes 1179648 | tf_op jit(solution)/shard_map/all_to_all | solution.py:40
  638.6 209.4 %all-gather.16.cloned.1.call-start = ((), (), s32[]{:S(2)}) async-start(), calls=%async_computation.28 | async-start | bytes 3981312 | tf_op jit(solution)/shard_map/all_gather | solution.py:73
  673.1 25.5 %all-to-all-start.7 = ((bf16[4,32,2304]{2,1,0:T(8,128)(2,1)}), bf16[4,32,2304]{2,1,0:T(8,128)(2,1)S(1)}, u32[]{:S(2)}, u32[]{:S(2)}) async-start(bf16[4,32,2304]{2,1,0:T(8,128)(2,1)} %broadcast_in_dim.22), calls=%async_computation.9 | async-start | bytes 1179648 | tf_op jit(solution)/shard_map/all_to_all | solution.py:40
  699.7 44.8 %all-to-all-start.14 = ((bf16[4,32,4608]{2,1,0:T(8,128)(2,1)}), bf16[4,32,4608]{2,1,0:T(8,128)(2,1)S(1)}, u32[]{:S(2)}, u32[]{:S(2)}) async-start(bf16[4,32,4608]{2,1,0:T(8,128)(2,1)} %broadcast_in_dim.27), calls=%async_computation.18 | async-start | bytes 2359296 | tf_op jit(solution)/shard_map/all_to_all | solution.py:40
  745.4 33.1 %all-to-all-start.8 = ((bf16[4,2,32,1152]{3,2,1,0:T(8,128)(2,1)}), bf16[4,2,32,1152]{3,2,1,0:T(8,128)(2,1)S(1)}, u32[]{:S(2)}, u32[]{:S(2)}) async-start(bf16[4,2,32,1152]{3,2,1,0:T(8,128)(2,1)} %broadcast_in_dim.23), calls=%async_computation.10 | async-start | bytes 1179648 | tf_op jit(solution)/shard_map/all_to_all | solution.py:40
  749.6 34.3 %collective-permute-start.13 = (bf16[4,32,2304]{2,1,0:T(8,128)(2,1)S(1)}, bf16[4,32,2304]{2,1,0:T(8,128)(2,1)}, u32[]{:S(2)}, u32[]{:S(2)}) collective-permute-start(bf16[4,32,2304]{2,1,0:T(8,128)(2,1)S(1)} %all-to-all-done.7), channel_id=1, source_target_pairs={{0,2},{2,0},{4,6},{6,4},{8,10},{10,8},{12,14},{14,12},{1,3},{3,1},... | collective-permute-start | bytes 1769480 | tf_op jit(solution)/shard_map/ppermute | solution.py:31
  751.0 58.2 %collective-permute-start.23 = (bf16[4,32,4608]{2,1,0:T(8,128)(2,1)S(1)}, bf16[4,32,4608]{2,1,0:T(8,128)(2,1)}, u32[]{:S(2)}, u32[]{:S(2)}) collective-permute-start(bf16[4,32,4608]{2,1,0:T(8,128)(2,1)S(1)} %all-to-all-done.14), channel_id=1, source_target_pairs={{0,2},{2,0},{4,6},{6,4},{8,10},{10,8},{12,14},{14,12},{1,3},{3,1},... | collective-permute-start | bytes 3538952 | tf_op jit(solution)/shard_map/ppermute | solution.py:31
  779.6 59.4 %all-to-all-start.15 = ((bf16[4,2,32,2304]{3,2,1,0:T(8,128)(2,1)}), bf16[4,2,32,2304]{3,2,1,0:T(8,128)(2,1)}, u32[]{:S(2)}, u32[]{:S(2)}) async-start(bf16[4,2,32,2304]{3,2,1,0:T(8,128)(2,1)} %broadcast_in_dim.28), calls=%async_computation.19 | async-start | bytes 2359296 | tf_op jit(solution)/shard_map/all_to_all | solution.py:40
  797.9 59.7 %collective-permute-start.15 = (bf16[256,640]{1,0:T(8,128)(2,1)S(1)}, bf16[256,640]{1,0:T(8,128)(2,1)}, u32[]{:S(2)}, u32[]{:S(2)}) collective-permute-start(bf16[256,640]{1,0:T(8,128)(2,1)S(1)} %fusion.101), channel_id=1, source_target_pairs={{0,16},{16,0},{1,17},{17,1},{2,18},{18,2},{3,19},{19,3},{4,20},{20... | collective-permute-start | bytes 983048 | tf_op jit(solution)/shard_map/ppermute | solution.py:31
  860.3 72.3 %collective-permute-start.26 = (bf16[256,640]{1,0:T(8,128)(2,1)S(1)}, bf16[256,640]{1,0:T(8,128)(2,1)S(1)}, u32[]{:S(2)}, u32[]{:S(2)}) collective-permute-start(bf16[256,640]{1,0:T(8,128)(2,1)S(1)} %add_convert_fusion), channel_id=1, source_target_pairs={{0,1},{1,0},{2,3},{3,2},{4,5},{5,4},{6,7},{7,6},{8,9},{9,8},{10,11... | collective-permute-start | bytes 983048 | tf_op jit(solution)/shard_map/ppermute | solution.py:31
  870.1 63.5 %all-to-all-start.9 = ((bf16[8,32,640]{2,1,0:T(8,128)(2,1)}), bf16[8,32,640]{2,1,0:T(8,128)(2,1)S(1)}, u32[]{:S(2)}, u32[]{:S(2)}) async-start(bf16[8,32,640]{2,1,0:T(8,128)(2,1)} %bitcast.42), calls=%async_computation.11 | async-start | bytes 655360 | tf_op jit(solution)/shard_map/all_to_all | solution.py:161
  (36 other events, 554.5 us)
Sparse Core Ops, SparseCore 0:
  53.1 111.9 reduce-scatter.4
  168.0 59.8 all-gather.9
  231.4 90.4 reduce-scatter.8
  325.4 92.0 reduce-scatter.6
  420.4 107.6 all-gather.13
  595.1 73.4 reduce-scatter.10
  671.6 61.6 all-gather.11
  735.7 104.4 all-gather.15

commit v2 on v1

v2 whole, which is shorter than its diff:
```python
import jax
import jax.numpy as jnp
from jax import lax
from jax.sharding import PartitionSpec as P

EPSILON = 1e-06
BF16 = jnp.bfloat16
F32 = jnp.float32
LANES = 128

GATE_SHARE = 1.0
UP_SHARE = 0.0
EARLY_HIDDEN_SHARE = 1.0
LATE_HIDDEN_SHARE = 1.0
EARLY_BACK_SHARE = 0.0
LATE_BACK_SHARE = 0.0
HOP_PIECES = 2


def cut(width, share):
    if share <= 0.0:
        return 0
    if share >= 1.0:
        return width
    whole = width // LANES
    return min(max(int(whole * share + 0.5), 1), whole - 1) * LANES


def pieces_of(low, high, count):
    units = (high - low) // LANES
    count = max(1, min(count, units))
    edges = [low + LANES * (units * i // count) for i in range(count)] + [high]
    return list(zip(edges[:-1], edges[1:]))


def contract_last(left, right):
    return lax.dot_general(left, right, (((1,), (1,)), ((), ())), preferred_element_type=F32)


def product(left, right):
    return jnp.dot(left, right, preferred_element_type=F32).astype(BF16)


def swap(value, axis, step=1):
    count = lax.axis_size(axis)
    return lax.ppermute(value, axis, [(i, i ^ step) for i in range(count)])


def line_exchange(value):
    count = lax.axis_size("dp")
    groups = [list(range(start, count, 2)) for start in range(2)]
    return lax.all_to_all(
        value, "dp", split_axis=0, concat_axis=0, tiled=True, axis_index_groups=groups
    )


def is_first_of_pair():
    return lax.axis_index("dp") % 2 == 0


def to_relative(value):
    count = lax.axis_size("dp")
    split = value.reshape((count // 2, 2, value.shape[0] // count) + value.shape[1:])
    flat = (value.shape[0] // 2,) + value.shape[1:]
    first, second = split[:, 0].reshape(flat), split[:, 1].reshape(flat)
    here = is_first_of_pair()
    return jnp.where(here, first, second), jnp.where(here, second, first)


def from_relative(own, other):
    count = lax.axis_size("dp")
    here = is_first_of_pair()
    shape = (count // 2, own.shape[0] // (count // 2)) + own.shape[1:]
    first = jnp.where(here, own, other).reshape(shape)
    second = jnp.where(here, other, own).reshape(shape)
    return jnp.stack([first, second], axis=1).reshape((2 * own.shape[0],) + own.shape[1:])


def scatter_product(multiply, values, width, share, marks=None, before=None):
    half_count = lax.axis_size("dp") // 2
    edge = cut(width, share)
    outs = []
    if edge > 0:
        part = multiply(values, 0, edge)
        if marks is not None:
            marks.append(part)
        if before is not None:
            part, before = lax.optimization_barrier((part, before))
        outs.append(lax.psum_scatter(part, "dp", scatter_dimension=0, tiled=True).astype(F32))
    if edge < width:
        own, other = to_relative(values)
        for low, high in pieces_of(edge, width, HOP_PIECES):
            given = multiply(other, low, high)
            kept = lax.optimization_barrier(multiply(own, low, high))
            if marks is not None:
                marks.append(kept)
            paired = (kept.astype(F32) + swap(given, "dp").astype(F32)).astype(BF16)
            lined = line_exchange(paired.reshape(half_count, -1, high - low))
            outs.append(jnp.sum(lined.astype(F32), axis=0))
    return jnp.concatenate(outs, axis=1) if len(outs) > 1 else outs[0]


def gather_contract(multiply, value, share, extra=None, first=None, marks=None):
    half_count = lax.axis_size("dp") // 2
    width = value.shape[1]
    edge = cut(width, share)
    total = None
    everyone = None
    if edge < width:
        own_total, other_total = None, None
        for low, high in pieces_of(edge, width, HOP_PIECES):
            part = value[:, low:high]
            if extra is not None and low == edge:
                part = jnp.concatenate([part, extra], axis=1)
            lined = line_exchange(jnp.broadcast_to(part[None], (half_count,) + part.shape))
            lined = lined.reshape(-1, part.shape[1])
            arrived = swap(lined, "dp")
            if extra is not None and low == edge:
                everyone = from_relative(lined[:, high - low :], arrived[:, high - low :])
                lined, arrived = lined[:, : high - low], arrived[:, : high - low]
            own_part = multiply(lined, low, high)
            if first is not None and high == width:
                arrived, first = lax.optimization_barrier((arrived, first))
            other_part = multiply(arrived, low, high)
            own_total = own_part if own_total is None else own_total + own_part
            other_total = other_part if other_total is None else other_total + other_part
        total = from_relative(own_total, other_total)
    if edge > 0:
        part = value[:, :edge]
        if extra is not None and edge == width:
            part = jnp.concatenate([part, extra], axis=1)
        called = lax.all_gather(part, "dp", axis=0, tiled=True)
        if marks is not None:
            marks.append(called)
        if extra is not None and edge == width:
            everyone = called[:, edge:]
        called = multiply(called[:, :edge], 0, edge)
        total = called if total is None else total + called
    if first is not None:
        total = total + first
    return total, everyone


def halving_sum(value, axis):
    step = 1
    while step < lax.axis_size(axis):
        value = value + swap(value, axis, step)
        step *= 2
    return value


def sum_shares(partial_value):
    total = partial_value.astype(BF16)
    total = (total.astype(F32) + swap(total, "segment").astype(F32)).astype(BF16)
    step = 1
    while step < lax.axis_size("tensor"):
        total = (total.astype(F32) + swap(total, "tensor", step).astype(F32)).astype(BF16)
        step *= 2
    return total.astype(F32)


def input_grads(d_hidden, stash_gate, stash_up):
    gate_pre = stash_gate.astype(F32)
    up_pre = stash_up.astype(F32)
    sigmoid_gate = jax.nn.sigmoid(gate_pre)
    d_gate = (d_hidden * up_pre * sigmoid_gate * (1.0 + gate_pre * (1.0 - sigmoid_gate))).astype(BF16)
    d_up = (d_hidden * gate_pre * sigmoid_gate).astype(BF16)
    return (d_gate, d_up)


def body(tokens, cotangent, gains, w_gate, w_up, w_down):
    gate_weight, up_weight, down_weight = w_gate[0], w_up[0], w_down[0]
    column_block, held = gate_weight.shape
    half = held // 2
    rows, features = tokens.shape
    segment = lax.axis_index("segment")
    block = lax.axis_index("dp")
    leading = segment == 0

    def other_half(weight, position):
        given = lax.dynamic_slice_in_dim(weight, (1 - position) * half, half, 1)
        return swap(given, "segment")

    def half_pick(own, other, early, function):
        def apply(value, low, high):
            first = lambda v, mine, theirs: function(v, mine, low, high)
            if early:
                return lax.cond(
                    leading, first, lambda v, m, t: function(v, t, low, high), value, own, other
                )
            return lax.cond(
                leading,
                lambda v, m, t: function(v, t, low, high),
                lambda v, m, t: function(v, m, half + low, half + high),
                value,
                own,
                other,
            )

        return apply

    def columns_product(value, weight, low, high):
        return product(value, weight[:, low:high])

    def columns_contract(value, weight, low, high):
        return contract_last(value, weight[:, low:high])

    def own_rows(value):
        return lax.dynamic_slice_in_dim(value, block * rows, rows, 0)

    def to_rows(value):
        return lax.all_to_all(value, "dp", split_axis=0, concat_axis=1, tiled=True)

    def row_inverse(cols):
        wide = cols.astype(F32)
        total = halving_sum(jnp.sum(wide * wide, axis=1), "dp")
        return lax.rsqrt(total[:, None] / features + EPSILON)

    gate_other = other_half(gate_weight, segment)
    up_other = other_half(up_weight, segment)
    mixed = lax.all_to_all(
        jnp.where(leading, tokens, cotangent), "dp", split_axis=1, concat_axis=0, tiled=True
    )
    mixed_other = swap(mixed, "segment")
    token_cols = jnp.where(leading, mixed, mixed_other)
    cotangent_cols = jnp.where(leading, mixed_other, mixed)
    gain_own = lax.dynamic_slice_in_dim(gains, block * column_block, column_block, 1)
    gain_other = swap(gain_own, "segment")
    early_gain = jnp.where(leading, gain_own, gain_other)
    late_gain = jnp.where(leading, gain_other, gain_own)

    def gate_and_up(early, cols, gain_row, marks=None):
        scaled = (cols.astype(F32) * gain_row).astype(BF16)
        gate = scatter_product(
            half_pick(gate_weight, gate_other, early, columns_product), scaled, half, GATE_SHARE, marks
        )
        up = scatter_product(
            half_pick(up_weight, up_other, early, columns_product), scaled, half, UP_SHARE, marks
        )
        return gate, up

    def hidden_of(gate, up):
        return (jax.nn.silu(gate) * up).astype(BF16)

    def back(early, d_hidden, gate, up):
        d_gate, d_up = input_grads(d_hidden, gate.astype(BF16), up.astype(BF16))
        share = jnp.sum(d_gate.astype(F32) * gate + d_up.astype(F32) * up, axis=1, keepdims=True)
        high = share.astype(BF16)
        low = (share - high.astype(F32)).astype(BF16)
        extra = jnp.pad(jnp.concatenate([high, low], axis=1), ((0, 0), (0, LANES - 2)))
        by_gate, _ = gather_contract(
            half_pick(gate_weight, gate_other, early, columns_contract), d_gate, GATE_SHARE
        )
        d_normed, everyone = gather_contract(
            half_pick(up_weight, up_other, early, columns_contract), d_up, UP_SHARE, extra, by_gate
        )
        shares = jnp.sum(everyone[:, :2].astype(F32), axis=1)
        mean_value = halving_sum(halving_sum(shares, "segment"), "tensor")[:, None] / features
        return d_normed, mean_value

    def norm_back(cols, inverse, gain_row, d_normed, mean_value, incoming):
        unit = cols.astype(F32) * inverse
        weighted = d_normed * gain_row
        return (incoming.astype(F32) + inverse * (weighted - unit * mean_value)).astype(BF16)

    inverse_in = row_inverse(token_cols)
    marks = []
    early_gate, early_up = gate_and_up(True, token_cols, early_gain, marks)
    after, _ = lax.optimization_barrier((segment, tuple(marks)))
    down_other = other_half(down_weight, after)
    late_d_hidden = scatter_product(
        half_pick(down_weight, down_other, False, columns_product),
        cotangent_cols,
        half,
        LATE_BACK_SHARE,
    )
    early_gate, early_up = early_gate * own_rows(inverse_in), early_up * own_rows(inverse_in)
    down_out, _ = gather_contract(
        half_pick(down_weight, down_other, True, columns_contract),
        hidden_of(early_gate, early_up),
        EARLY_HIDDEN_SHARE,
    )
    early_out = (token_cols.astype(F32) + sum_shares(down_out)).astype(BF16)
    early_out, late_d_hidden = lax.optimization_barrier((early_out, late_d_hidden))

    inverse_mid = row_inverse(early_out)
    late_gate, late_up = gate_and_up(False, early_out, late_gain)
    late_gate, late_up = late_gate * own_rows(inverse_mid), late_up * own_rows(inverse_mid)
    d_normed, mean_value = back(False, late_d_hidden, late_gate, late_up)
    down_out, _ = gather_contract(
        half_pick(down_weight, down_other, False, columns_contract),
        hidden_of(late_gate, late_up),
        LATE_HIDDEN_SHARE,
        marks=marks,
    )
    d_early = norm_back(
        early_out, inverse_mid, late_gain, sum_shares(d_normed), mean_value, cotangent_cols
    )
    late_out = (early_out.astype(F32) + sum_shares(down_out)).astype(BF16)
    acts = to_rows(jnp.where(leading, early_out, late_out))[None]

    d_hidden = scatter_product(
        half_pick(down_weight, down_other, True, columns_product),
        d_early,
        half,
        EARLY_BACK_SHARE,
        before=marks[-1],
    )
    d_normed, mean_value = back(True, d_hidden, early_gate, early_up)
    d_tokens = norm_back(
        token_cols, inverse_in, early_gain, sum_shares(d_normed), mean_value, d_early
    )
    grads = to_rows(jnp.where(leading, d_tokens, d_early))[None]
    return (acts, grads)


def solution(mesh):
    in_specs = (
        P("dp", None),
        P("dp", None),
        P("segment", None),
        P("segment", "dp", "tensor"),
        P("segment", "dp", "tensor"),
        P("segment", "dp", "tensor"),
    )
    out_specs = (P("segment", "dp", None), P("segment", "dp", None))
    return jax.shard_map(body, mesh=mesh, in_specs=in_specs, out_specs=out_specs, check_vma=False)
```

time: 969 us -> 802 us (0.83)
  waiting for transfers between devices: 489 us -> 374 us
  blocking collectives: 159 us -> 96.9 us
  matrix products: 104 us -> 138 us
  starting transfers between devices: 96.6 us -> 82.4 us
  local copies, waits for them, and re-layouts: 54.7 us -> 41.6 us
    all_to_all x14 -> x10, waiting for transfers between devices: 267 us -> 138 us  [line_exchange(): lax.all_to_all(value, 'dp', split_axis=0, concat_axis=0, tiled=True, axis...]
    unnamed x3 -> x0, blocking collectives: 99.5 us -> none
    all_to_all x0 -> x2, blocking collectives: none -> 78.8 us  [line_exchange(): lax.all_to_all(value, 'dp', split_axis=0, concat_axis=0, tiled=True, axis...]
    ppermute x27 -> x35, waiting for transfers between devices: 165 us -> 227 us  [swap(): return lax.ppermute(value, axis, [(i, i ^ step) for i in range(count)])]
    reduce_scatter x4 -> x2, waiting for transfers between devices: 48.2 us -> 0.04 us  [scatter_product(): lax.psum_scatter(part, 'dp', scatter_dimension=0, tiled=True).astype(F32)]
    all_gather x1 -> x0, blocking collectives: 41.2 us -> none  [body(): squares = lax.all_gather(jnp.sum(wide_mid * wide_mid, axis=1), 'dp')]
    dot_general x7 -> x18, matrix products: 51.1 us -> 73.1 us  [product(): return jnp.dot(left, right, preferred_element_type=F32).astype(BF16)]
    all_to_all x14 -> x10, starting transfers between devices: 53.9 us -> 38.4 us  [line_exchange(): lax.all_to_all(value, 'dp', split_axis=0, concat_axis=0, tiled=True, axis...]
  transfers between devices with their start and end apart: 51 -> 53, of which waited for: 32 -> 31; matrix products, arithmetic and copies ran while one was open for 17% -> 24% of each run, Pallas kernels for 0% -> 0%
where the time goes in v2:
time: 802 us; the launch traced here: 791 us
  waiting for transfers between devices  374 us (47%)
  matrix products  138 us (17%)
  blocking collectives  96.9 us (12%)
  starting transfers between devices  82.4 us (10%)
  local copies, waits for them, and re-layouts  41.6 us (5%)
  other arithmetic  41.2 us (5%)
  between operations  15.4 us (2%)
    ppermute x35, waiting for transfers between devices, swap(): return lax.ppermute(value, axis, [(i, i ^ step) for i in range(count)])  227 us
    all_to_all x10, waiting for transfers between devices, line_exchange(): lax.all_to_all(value, 'dp', split_axis=0, concat_axis=0, tiled=True, axis...  138 us
    all_to_all x2, blocking collectives, line_exchange(): lax.all_to_all(value, 'dp', split_axis=0, concat_axis=0, tiled=True, axis...  78.8 us
    dot_general x18, matrix products, product(): return jnp.dot(left, right, preferred_element_type=F32).astype(BF16)  73.1 us
    dot_general x12, matrix products, contract_last(): lax.dot_general(left, right, (((1,), (1,)), ((), ())), preferred_element_...  65.1 us
    all_to_all x10, starting transfers between devices, line_exchange(): lax.all_to_all(value, 'dp', split_axis=0, concat_axis=0, tiled=True, axis...  38.4 us
    ppermute x35, starting transfers between devices, swap(): return lax.ppermute(value, axis, [(i, i ^ step) for i in range(count)])  33.8 us
    dynamic_slice x3, local copies, waits for them, and re-layouts, other_half(): given = lax.dynamic_slice_in_dim(weight, (1 - position) * half, half, 1)  23.3 us
  transfers between devices with their start and end apart: 53, of which 31 were waited for; matrix products, arithmetic and copies ran while one was open for 24% of the time, Pallas kernels for 0%

profile of v2, /device:TPU:0, one launch (start us, length us, event | category | flops | bytes accessed | tf_op | source)
XLA Modules:
  0.0 791.0 jit_solution(7949873702377975844)
XLA Ops:
  7.2 7.6 dynamic-slice_bitcast_fusion.2
  22.9 18.2 %all_to_all.111 = bf16[32,8,640]{2,0,1:T(8,128)(2,1)S(1)} all-to-all(bf16[32,8,640]{2,0,1:T(8,128)(2,1)S(1)} %bitcast.197), channel_id=1, replica_groups=mesh['segment'=2,'dp'=8,'tensor'=2] {'dp'}, dimensions={1} | all-to-all | bytes 655360 | tf_op jit(solution)/shard_map/all_to_all | solution.py:221
  44.4 8.2 %conditional.48 = (bf16[256,6912]{1,0:T(8,128)(2,1)}) conditional(s32[]{:T(128)} %convert_element_type.494, (bf16[256,640]{1,0:T(8,128)(2,1)S(1)}, bf16[640,6912]{1,0:T(8,128)(2,1)}) %tuple.246, (bf16[640,13824]{1,0:T(8,128)(2,1)}, bf16[256,640]{1,0:T(8,128)(2,1)S(1)}) %tuple.395), branch_computations={%region_0.1_spmd, %region_1.2_spmd} | conditional | flops 2264924160 | bytes 12713992
  44.4 8.2 %fusion = bf16[256,6912]{1,0:T(8,128)(2,1)} fusion(bf16[256,640]{1,0:T(8,128)(2,1)S(1)} %get-tuple-element.368, bf16[640,13824]{1,0:T(8,128)(2,1)} %get-tuple-element.369), kind=kOutput, calls=%fused_computation | convolution fusion | flops 2264924160 | bytes 12713984 | tf_op jit(solution)/shard_map/cond/branch_1_fun/dot_general | solution.py:41
  59.9 8.2 %dynamic-slice_bitcast_fusion = bf16[640,6912]{1,0:T(8,128)(2,1)} fusion(bf16[1,640,13824]{2,1,0:T(8,128)(2,1)} %param.71, s32[]{:T(128)S(6)} %select_n.192), kind=kLoop, calls=%fused_computation.108 | loop fusion | bytes 17694724 | tf_op jit(solution)/shard_map/dynamic_slice | solution.py:181
  78.6 25.8 %collective-permute-done.8 = bf16[128,3456]{1,0:T(8,128)(2,1)S(1)} collective-permute-done((bf16[128,3456]{1,0:T(8,128)(2,1)}, bf16[128,3456]{1,0:T(8,128)(2,1)S(1)}, u32[]{:S(2)}, u32[]{:S(2)}) %collective-permute-start.8) | collective-permute-done | bytes 884768 | tf_op jit(solution)/shard_map/ppermute | solution.py:46
  111.1 16.6 %collective-permute-done.7 = bf16[128,3456]{1,0:T(8,128)(2,1)S(1)} collective-permute-done((bf16[128,3456]{1,0:T(8,128)(2,1)}, bf16[128,3456]{1,0:T(8,128)(2,1)S(1)}, u32[]{:S(2)}, u32[]{:S(2)}) %collective-permute-start.7) | collective-permute-done | bytes 884768 | tf_op jit(solution)/shard_map/ppermute | solution.py:46
  130.1 11.0 %all-to-all-done.2 = bf16[4,32,3456]{2,1,0:T(8,128)(2,1)S(1)} async-done(((bf16[4,32,3456]{2,1,0:T(8,128)(2,1)}), bf16[4,32,3456]{2,1,0:T(8,128)(2,1)S(1)}, u32[]{:S(2)}, u32[]{:S(2)}) %all-to-all-start.2) | async-done | bytes 884768 | tf_op jit(solution)/shard_map/all_to_all | solution.py:52
  150.2 9.1 %collective-permute-done.4 = f32[256]{0:T(256)S(1)} collective-permute-done((f32[256]{0:T(256)S(1)}, f32[256]{0:T(256)S(1)}, u32[]{:S(2)}, u32[]{:S(2)}) %collective-permute-start.4) | collective-permute-done | bytes 1056 | tf_op jit(solution)/shard_map/ppermute | solution.py:46
  184.5 17.1 %collective-permute-done.13 = bf16[128,3456]{1,0:T(8,128)(2,1)S(1)} collective-permute-done((bf16[128,3456]{1,0:T(8,128)(2,1)}, bf16[128,3456]{1,0:T(8,128)(2,1)S(1)}, u32[]{:S(2)}, u32[]{:S(2)}) %collective-permute-start.13) | collective-permute-done | bytes 884768 | tf_op jit(solution)/shard_map/ppermute | solution.py:46
  211.7 23.4 %collective-permute-done.12 = bf16[128,3456]{1,0:T(8,128)(2,1)S(1)} collective-permute-done((bf16[128,3456]{1,0:T(8,128)(2,1)}, bf16[128,3456]{1,0:T(8,128)(2,1)S(1)}, u32[]{:S(2)}, u32[]{:S(2)}) %collective-permute-start.12) | collective-permute-done | bytes 884768 | tf_op jit(solution)/shard_map/ppermute | solution.py:46
  237.5 13.0 %all-to-all-done.4 = bf16[4,32,3456]{2,1,0:T(8,128)(2,1)S(1)} async-done(((bf16[4,32,3456]{2,1,0:T(8,128)(2,1)}), bf16[4,32,3456]{2,1,0:T(8,128)(2,1)S(1)}, u32[]{:S(2)}, u32[]{:S(2)}) %all-to-all-start.4) | async-done | bytes 884768 | tf_op jit(solution)/shard_map/all_to_all | solution.py:52
  254.1 7.8 conditional.53
  263.5 11.6 %all-to-all-done.3 = bf16[4,32,3456]{2,1,0:T(8,128)(2,1)S(1)} async-done(((bf16[4,32,3456]{2,1,0:T(8,128)(2,1)}), bf16[4,32,3456]{2,1,0:T(8,128)(2,1)S(1)}, u32[]{:S(2)}, u32[]{:S(2)}) %all-to-all-start.3) | async-done | bytes 884768 | tf_op jit(solution)/shard_map/all_to_all | solution.py:52
  285.3 7.9 conditional.112
  285.4 7.9 fusion.164
  308.3 20.9 %collective-permute-done.18 = bf16[128,3456]{1,0:T(8,128)(2,1)S(1)} collective-permute-done((bf16[128,3456]{1,0:T(8,128)(2,1)}, bf16[128,3456]{1,0:T(8,128)(2,1)S(1)}, u32[]{:S(2)}, u32[]{:S(2)}) %collective-permute-start.18) | collective-permute-done | bytes 884768 | tf_op jit(solution)/shard_map/ppermute | solution.py:46
  339.2 14.0 %collective-permute-done.17 = bf16[128,3456]{1,0:T(8,128)(2,1)S(1)} collective-permute-done((bf16[128,3456]{1,0:T(8,128)(2,1)}, bf16[128,3456]{1,0:T(8,128)(2,1)S(1)}, u32[]{:S(2)}, u32[]{:S(2)}) %collective-permute-start.17) | collective-permute-done | bytes 884768 | tf_op jit(solution)/shard_map/ppermute | solution.py:46
  364.6 18.6 %collective-permute-done.15 = f32[256]{0:T(256)S(1)} collective-permute-done((f32[256]{0:T(256)S(1)}, f32[256]{0:T(256)S(1)}, u32[]{:S(2)}, u32[]{:S(2)}) %collective-permute-start.15) | collective-permute-done | bytes 1056 | tf_op jit(solution)/shard_map/ppermute | solution.py:46
  384.7 10.1 %collective-permute-done.16 = f32[256]{0:T(256)S(1)} collective-permute-done((f32[256]{0:T(256)S(1)}, f32[256]{0:T(256)S(1)}, u32[]{:S(2)}, u32[]{:S(2)}) %collective-permute-start.16) | collective-permute-done | bytes 1056 | tf_op jit(solution)/shard_map/ppermute | solution.py:46
  399.5 39.7 %all_to_all.112 = bf16[4,32,3584]{2,1,0:T(8,128)(2,1)S(1)} all-to-all(bf16[4,32,3584]{2,1,0:T(8,128)(2,1)S(1)} %broadcast_in_dim.13), channel_id=1, replica_groups={{0,4,8,12},{2,6,10,14},{1,5,9,13},{3,7,11,15},{16,20,24,28},{18,22,26,3..., dimensions={0} | all-to-all | bytes 1835008 | tf_op jit(solution)/shard_map/all_to_all | solution.py:52
  446.7 37.4 %all-to-all-done.9 = bf16[4,32,3456]{2,1,0:T(8,128)(2,1)} async-done(((bf16[4,32,3456]{2,1,0:T(8,128)(2,1)}), bf16[4,32,3456]{2,1,0:T(8,128)(2,1)}, u32[]{:S(2)}, u32[]{:S(2)}) %all-to-all-start.9) | async-done | bytes 884768 | tf_op jit(solution)/shard_map/all_to_all | solution.py:52
  502.2 8.1 %conditional.121 = (f32[256,640]{1,0:T(8,128)S(1)}) conditional(s32[]{:T(128)} %convert_element_type.494, (bf16[640,13824]{1,0:T(8,128)(2,1)}, bf16[256,6912]{1,0:T(8,128)(2,1)}) %tuple.397, (bf16[256,6912]{1,0:T(8,128)(2,1)}, bf16[640,6912]{1,0:T(8,128)(2,1)}) %tuple.275), branch_computations={%region_49.50_spmd, %region_50.51_spmd} | conditional | flops 2264924160 | bytes 13041672 | solution.py:191
  502.4 8.0 %fusion.166 = f32[256,640]{1,0:T(8,128)S(1)} fusion(bf16[256,6912]{1,0:T(8,128)(2,1)} %get-tuple-element.444, bf16[640,6912]{1,0:T(8,128)(2,1)} %get-tuple-element.445), kind=kOutput, calls=%fused_computation.255 | convolution fusion | flops 2264924160 | bytes 13041664 | tf_op jit(solution)/shard_map/cond/branch_1_fun/dot_general | solution.py:37
  543.7 24.5 %collective-permute-done.28 = bf16[128,3456]{1,0:T(8,128)(2,1)S(1)} collective-permute-done((bf16[128,3456]{1,0:T(8,128)(2,1)}, bf16[128,3456]{1,0:T(8,128)(2,1)S(1)}, u32[]{:S(2)}, u32[]{:S(2)}) %collective-permute-start.28) | collective-permute-done | bytes 884768 | tf_op jit(solution)/shard_map/ppermute | solution.py:46
  588.8 7.7 all-to-all-done.11
  601.0 20.7 %all-to-all-done.10 = bf16[4,32,3456]{2,1,0:T(8,128)(2,1)S(1)} async-done(((bf16[4,32,3456]{2,1,0:T(8,128)(2,1)}), bf16[4,32,3456]{2,1,0:T(8,128)(2,1)S(1)}, u32[]{:S(2)}, u32[]{:S(2)}) %all-to-all-start.10) | async-done | bytes 884768 | tf_op jit(solution)/shard_map/all_to_all | solution.py:52
  624.8 39.0 %all_to_all.113 = bf16[4,32,3584]{2,1,0:T(8,128)(2,1)S(1)} all-to-all(bf16[4,32,3584]{2,1,0:T(8,128)(2,1)S(1)} %broadcast_in_dim.15), channel_id=1, replica_groups={{0,4,8,12},{2,6,10,14},{1,5,9,13},{3,7,11,15},{16,20,24,28},{18,22,26,3..., dimensions={0} | all-to-all | bytes 1835008 | tf_op jit(solution)/shard_map/all_to_all | solution.py:52
  669.2 7.6 conditional.117
  669.2 7.5 fusion.165
  677.5 36.4 %all-to-all-done.13 = bf16[4,32,3456]{2,1,0:T(8,128)(2,1)} async-done(((bf16[4,32,3456]{2,1,0:T(8,128)(2,1)}), bf16[4,32,3456]{2,1,0:T(8,128)(2,1)}, u32[]{:S(2)}, u32[]{:S(2)}) %all-to-all-start.13) | async-done | bytes 884768 | tf_op jit(solution)/shard_map/all_to_all | solution.py:52
  774.1 8.7 %all-to-all-done.14 = bf16[8,32,640]{2,1,0:T(8,128)(2,1)S(1)} async-done(((bf16[8,32,640]{2,1,0:T(8,128)(2,1)}), bf16[8,32,640]{2,1,0:T(8,128)(2,1)S(1)}, u32[]{:S(2)}, u32[]{:S(2)}) %all-to-all-start.14) | async-done | bytes 327712 | tf_op jit(solution)/shard_map/all_to_all | solution.py:212
  (284 shorter events, 403.2 us)
Async XLA Ops:
  7.2 159.7 %reduce-scatter.3.cloned.1.call-start = ((), (), s32[]{:S(2)}) async-start(), calls=%async_computation.17 | async-start | bytes 3981312 | tf_op jit(solution)/shard_map/reduce_scatter | solution.py:89
  14.8 29.3 %collective-permute-start.2 = (bf16[640,6912]{1,0:T(8,128)(2,1)}, bf16[640,6912]{1,0:T(8,128)(2,1)}, u32[]{:S(2)}, u32[]{:S(2)}) collective-permute-start(bf16[640,6912]{1,0:T(8,128)(2,1)} %dynamic-slice_bitcast_fusion.2), channel_id=1, source_target_pairs={{0,16},{16,0},{1,17},{17,1},{2,18},{18,2},{3,19},{19,3},{4,20},{20... | collective-permute-start | bytes 26542088 | tf_op jit(solution)/shard_map/ppermute | solution.py:46
  22.7 29.9 %collective-permute-start.6 = (bf16[640,6912]{1,0:T(8,128)(2,1)}, bf16[640,6912]{1,0:T(8,128)(2,1)}, u32[]{:S(2)}, u32[]{:S(2)}) collective-permute-start(bf16[640,6912]{1,0:T(8,128)(2,1)} %dynamic-slice_bitcast_fusion.1), channel_id=1, source_target_pairs={{0,16},{16,0},{1,17},{17,1},{2,18},{18,2},{3,19},{19,3},{4,20},{20... | collective-permute-start | bytes 26542088 | tf_op jit(solution)/shard_map/ppermute | solution.py:46
  68.1 101.8 %collective-permute-start.9 = (bf16[640,6912]{1,0:T(8,128)(2,1)}, bf16[640,6912]{1,0:T(8,128)(2,1)}, u32[]{:S(2)}, u32[]{:S(2)}) collective-permute-start(bf16[640,6912]{1,0:T(8,128)(2,1)} %dynamic-slice_bitcast_fusion), channel_id=1, source_target_pairs={{0,16},{16,0},{1,17},{17,1},{2,18},{18,2},{3,19},{19,3},{4,20},{20... | collective-permute-start | bytes 26542088 | tf_op jit(solution)/shard_map/ppermute | solution.py:46
  72.3 32.1 %collective-permute-start.8 = (bf16[128,3456]{1,0:T(8,128)(2,1)}, bf16[128,3456]{1,0:T(8,128)(2,1)S(1)}, u32[]{:S(2)}, u32[]{:S(2)}) collective-permute-start(bf16[128,3456]{1,0:T(8,128)(2,1)} %get-tuple-element.539), channel_id=1, source_target_pairs={{0,2},{2,0},{4,6},{6,4},{8,10},{10,8},{12,14},{14,12},{1,3},{3,1},... | collective-permute-start | bytes 2654216 | tf_op jit(solution)/shard_map/ppermute | solution.py:46
  78.1 49.6 %collective-permute-start.7 = (bf16[128,3456]{1,0:T(8,128)(2,1)}, bf16[128,3456]{1,0:T(8,128)(2,1)S(1)}, u32[]{:S(2)}, u32[]{:S(2)}) collective-permute-start(bf16[128,3456]{1,0:T(8,128)(2,1)} %copy-done.20), channel_id=1, source_target_pairs={{0,2},{2,0},{4,6},{6,4},{8,10},{10,8},{12,14},{14,12},{1,3},{3,1},... | collective-permute-start | bytes 2654216 | tf_op jit(solution)/shard_map/ppermute | solution.py:46
  106.8 34.3 %all-to-all-start.2 = ((bf16[4,32,3456]{2,1,0:T(8,128)(2,1)}), bf16[4,32,3456]{2,1,0:T(8,128)(2,1)S(1)}, u32[]{:S(2)}, u32[]{:S(2)}) async-start(bf16[4,32,3456]{2,1,0:T(8,128)(2,1)} %bitcast.11), calls=%async_computation.3 | async-start | bytes 1769472 | tf_op jit(solution)/shard_map/all_to_all | solution.py:52
  141.1 25.6 %all-to-all-start.1 = ((bf16[4,32,3456]{2,1,0:T(8,128)(2,1)}), bf16[4,32,3456]{2,1,0:T(8,128)(2,1)S(1)}, u32[]{:S(2)}, u32[]{:S(2)}) async-start(bf16[4,32,3456]{2,1,0:T(8,128)(2,1)} %bitcast.181), calls=%async_computation.2 | async-start | bytes 1769472 | tf_op jit(solution)/shard_map/all_to_all | solution.py:52
  144.6 109.4 %all-gather.5.cloned.1.call-start = ((), (), s32[]{:S(2)}) async-start(), calls=%async_computation.18 | async-start | bytes 3981312 | tf_op jit(solution)/shard_map/all_gather | solution.py:132
  174.0 27.6 %collective-permute-start.13 = (bf16[128,3456]{1,0:T(8,128)(2,1)}, bf16[128,3456]{1,0:T(8,128)(2,1)S(1)}, u32[]{:S(2)}, u32[]{:S(2)}) collective-permute-start(bf16[128,3456]{1,0:T(8,128)(2,1)} %copy-done.21), channel_id=1, source_target_pairs={{0,2},{2,0},{4,6},{6,4},{8,10},{10,8},{12,14},{14,12},{1,3},{3,1},... | collective-permute-start | bytes 2654216 | tf_op jit(solution)/shard_map/ppermute | solution.py:46
  183.6 51.5 %collective-permute-start.12 = (bf16[128,3456]{1,0:T(8,128)(2,1)}, bf16[128,3456]{1,0:T(8,128)(2,1)S(1)}, u32[]{:S(2)}, u32[]{:S(2)}) collective-permute-start(bf16[128,3456]{1,0:T(8,128)(2,1)} %copy-done.22), channel_id=1, source_target_pairs={{0,2},{2,0},{4,6},{6,4},{8,10},{10,8},{12,14},{14,12},{1,3},{3,1},... | collective-permute-start | bytes 2654216 | tf_op jit(solution)/shard_map/ppermute | solution.py:46
  204.1 46.4 %all-to-all-start.4 = ((bf16[4,32,3456]{2,1,0:T(8,128)(2,1)}), bf16[4,32,3456]{2,1,0:T(8,128)(2,1)S(1)}, u32[]{:S(2)}, u32[]{:S(2)}) async-start(bf16[4,32,3456]{2,1,0:T(8,128)(2,1)} %bitcast.18), calls=%async_computation.5 | async-start | bytes 1769472 | tf_op jit(solution)/shard_map/all_to_all | solution.py:52
  250.5 24.6 %all-to-all-start.3 = ((bf16[4,32,3456]{2,1,0:T(8,128)(2,1)}), bf16[4,32,3456]{2,1,0:T(8,128)(2,1)S(1)}, u32[]{:S(2)}, u32[]{:S(2)}) async-start(bf16[4,32,3456]{2,1,0:T(8,128)(2,1)} %bitcast.183), calls=%async_computation.4 | async-start | bytes 1769472 | tf_op jit(solution)/shard_map/all_to_all | solution.py:52
  254.0 142.0 %reduce-scatter.5.cloned.1.call-start = ((), (), s32[]{:S(2)}) async-start(), calls=%async_computation.19 | async-start | bytes 3981312 | tf_op jit(solution)/shard_map/reduce_scatter | solution.py:89
  297.4 31.8 %collective-permute-start.18 = (bf16[128,3456]{1,0:T(8,128)(2,1)}, bf16[128,3456]{1,0:T(8,128)(2,1)S(1)}, u32[]{:S(2)}, u32[]{:S(2)}) collective-permute-start(bf16[128,3456]{1,0:T(8,128)(2,1)} %copy-done.23), channel_id=1, source_target_pairs={{0,2},{2,0},{4,6},{6,4},{8,10},{10,8},{12,14},{14,12},{1,3},{3,1},... | collective-permute-start | bytes 2654216 | tf_op jit(solution)/shard_map/ppermute | solution.py:46
  307.2 46.0 %collective-permute-start.17 = (bf16[128,3456]{1,0:T(8,128)(2,1)}, bf16[128,3456]{1,0:T(8,128)(2,1)S(1)}, u32[]{:S(2)}, u32[]{:S(2)}) collective-permute-start(bf16[128,3456]{1,0:T(8,128)(2,1)} %get-tuple-element.547), channel_id=1, source_target_pairs={{0,2},{2,0},{4,6},{6,4},{8,10},{10,8},{12,14},{14,12},{1,3},{3,1},... | collective-permute-start | bytes 2654216 | tf_op jit(solution)/shard_map/ppermute | solution.py:46
  355.5 40.3 %all-to-all-start.5 = ((bf16[4,32,3456]{2,1,0:T(8,128)(2,1)}), bf16[4,32,3456]{2,1,0:T(8,128)(2,1)S(1)}, u32[]{:S(2)}, u32[]{:S(2)}) async-start(bf16[4,32,3456]{2,1,0:T(8,128)(2,1)} %bitcast.182), calls=%async_computation.7 | async-start | bytes 1769472 | tf_op jit(solution)/shard_map/all_to_all | solution.py:52
  359.0 143.2 %all-gather.9.cloned.1.call-start = ((), (), s32[]{:S(2)}) async-start(), calls=%async_computation.21 | async-start | bytes 3981312 | tf_op jit(solution)/shard_map/all_gather | solution.py:132
  440.2 43.9 %all-to-all-start.9 = ((bf16[4,32,3456]{2,1,0:T(8,128)(2,1)}), bf16[4,32,3456]{2,1,0:T(8,128)(2,1)}, u32[]{:S(2)}, u32[]{:S(2)}) async-start(bf16[4,32,3456]{2,1,0:T(8,128)(2,1)} %broadcast_in_dim.14), calls=%async_computation.11 | async-start | bytes 1769472 | tf_op jit(solution)/shard_map/all_to_all | solution.py:52
  444.4 224.8 %all-gather.7.cloned.1.call-start = ((), (), s32[]{:S(2)}) async-start(), calls=%async_computation.20 | async-start | bytes 3981312 | tf_op jit(solution)/shard_map/all_gather | solution.py:132
  444.4 52.4 %collective-permute-start.21 = (bf16[128,3584]{1,0:T(8,128)(2,1)S(1)}, bf16[128,3584]{1,0:T(8,128)(2,1)S(1)}, u32[]{:S(2)}, u32[]{:S(2)}) collective-permute-start(bf16[128,3584]{1,0:T(8,128)(2,1)S(1)} %bitcast.178), channel_id=1, source_target_pairs={{0,2},{2,0},{4,6},{6,4},{8,10},{10,8},{12,14},{14,12},{1,3},{3,1},... | collective-permute-start | bytes 2752520 | tf_op jit(solution)/shard_map/ppermute | solution.py:46
  484.1 26.3 %collective-permute-start.22 = (bf16[128,3456]{1,0:T(8,128)(2,1)}, bf16[128,3456]{1,0:T(8,128)(2,1)}, u32[]{:S(2)}, u32[]{:S(2)}) collective-permute-start(bf16[128,3456]{1,0:T(8,128)(2,1)} %bitcast.28), channel_id=1, source_target_pairs={{0,2},{2,0},{4,6},{6,4},{8,10},{10,8},{12,14},{14,12},{1,3},{3,1},... | collective-permute-start | bytes 2654216 | tf_op jit(solution)/shard_map/ppermute | solution.py:46
  533.5 34.6 %collective-permute-start.28 = (bf16[128,3456]{1,0:T(8,128)(2,1)}, bf16[128,3456]{1,0:T(8,128)(2,1)S(1)}, u32[]{:S(2)}, u32[]{:S(2)}) collective-permute-start(bf16[128,3456]{1,0:T(8,128)(2,1)} %get-tuple-element.559), channel_id=1, source_target_pairs={{0,2},{2,0},{4,6},{6,4},{8,10},{10,8},{12,14},{14,12},{1,3},{3,1},... | collective-permute-start | bytes 2654216 | tf_op jit(solution)/shard_map/ppermute | solution.py:46
  541.6 44.9 %collective-permute-start.27 = (bf16[128,3456]{1,0:T(8,128)(2,1)}, bf16[128,3456]{1,0:T(8,128)(2,1)S(1)}, u32[]{:S(2)}, u32[]{:S(2)}) collective-permute-start(bf16[128,3456]{1,0:T(8,128)(2,1)} %get-tuple-element.557), channel_id=1, source_target_pairs={{0,2},{2,0},{4,6},{6,4},{8,10},{10,8},{12,14},{14,12},{1,3},{3,1},... | collective-permute-start | bytes 2654216 | tf_op jit(solution)/shard_map/ppermute | solution.py:46
  570.4 26.1 %all-to-all-start.11 = ((bf16[4,32,3456]{2,1,0:T(8,128)(2,1)}), bf16[4,32,3456]{2,1,0:T(8,128)(2,1)S(1)}, u32[]{:S(2)}, u32[]{:S(2)}) async-start(bf16[4,32,3456]{2,1,0:T(8,128)(2,1)} %bitcast.39), calls=%async_computation.13 | async-start | bytes 1769472 | tf_op jit(solution)/shard_map/all_to_all | solution.py:52
  596.5 25.2 %all-to-all-start.10 = ((bf16[4,32,3456]{2,1,0:T(8,128)(2,1)}), bf16[4,32,3456]{2,1,0:T(8,128)(2,1)S(1)}, u32[]{:S(2)}, u32[]{:S(2)}) async-start(bf16[4,32,3456]{2,1,0:T(8,128)(2,1)} %bitcast.184), calls=%async_computation.12 | async-start | bytes 1769472 | tf_op jit(solution)/shard_map/all_to_all | solution.py:52
  600.0 139.8 %all-gather.11.cloned.1.call-start = ((), (), s32[]{:S(2)}) async-start(), calls=%async_computation.22 | async-start | bytes 3981312 | tf_op jit(solution)/shard_map/all_gather | solution.py:132
  664.9 49.1 %all-to-all-start.13 = ((bf16[4,32,3456]{2,1,0:T(8,128)(2,1)}), bf16[4,32,3456]{2,1,0:T(8,128)(2,1)}, u32[]{:S(2)}, u32[]{:S(2)}) async-start(bf16[4,32,3456]{2,1,0:T(8,128)(2,1)} %broadcast_in_dim.16), calls=%async_computation.15 | async-start | bytes 1769472 | tf_op jit(solution)/shard_map/all_to_all | solution.py:52
  676.8 37.8 %collective-permute-start.19 = (bf16[256,640]{1,0:T(8,128)(2,1)S(1)}, bf16[256,640]{1,0:T(8,128)(2,1)S(1)}, u32[]{:S(2)}, u32[]{:S(2)}) collective-permute-start(bf16[256,640]{1,0:T(8,128)(2,1)S(1)} %get-tuple-element.550), channel_id=1, source_target_pairs={{0,16},{16,0},{1,17},{17,1},{2,18},{18,2},{3,19},{19,3},{4,20},{20... | collective-permute-start | bytes 983048 | tf_op jit(solution)/shard_map/ppermute | solution.py:46
  676.8 58.2 %collective-permute-start.29 = (bf16[128,3584]{1,0:T(8,128)(2,1)S(1)}, bf16[128,3584]{1,0:T(8,128)(2,1)S(1)}, u32[]{:S(2)}, u32[]{:S(2)}) collective-permute-start(bf16[128,3584]{1,0:T(8,128)(2,1)S(1)} %bitcast.175), channel_id=1, source_target_pairs={{0,2},{2,0},{4,6},{6,4},{8,10},{10,8},{12,14},{14,12},{1,3},{3,1},... | collective-permute-start | bytes 2752520 | tf_op jit(solution)/shard_map/ppermute | solution.py:46
  714.0 34.0 %collective-permute-start.30 = (bf16[128,3456]{1,0:T(8,128)(2,1)}, bf16[128,3456]{1,0:T(8,128)(2,1)}, u32[]{:S(2)}, u32[]{:S(2)}) collective-permute-start(bf16[128,3456]{1,0:T(8,128)(2,1)} %bitcast.42), channel_id=1, source_target_pairs={{0,2},{2,0},{4,6},{6,4},{8,10},{10,8},{12,14},{14,12},{1,3},{3,1},... | collective-permute-start | bytes 2654216 | tf_op jit(solution)/shard_map/ppermute | solution.py:46
  722.7 44.4 %all-to-all-start.7 = ((bf16[8,32,640]{2,1,0:T(8,128)(2,1)}), bf16[8,32,640]{2,1,0:T(8,128)(2,1)S(1)}, u32[]{:S(2)}, u32[]{:S(2)}) async-start(bf16[8,32,640]{2,1,0:T(8,128)(2,1)} %bitcast.24), calls=%async_computation.9 | async-start | bytes 655360 | tf_op jit(solution)/shard_map/all_to_all | solution.py:212
  (45 other events, 264.5 us)
Sparse Core Ops, SparseCore 0:
  52.7 101.2 reduce-scatter.2
  169.2 83.8 all-gather.4
  293.4 101.4 reduce-scatter.4
  399.3 96.7 all-gather.8
  498.2 78.4 all-gather.6
  624.6 93.2 all-gather.10

commit v3 on v2

--- a/solution.py
+++ b/solution.py
@@ -91,6 +91,7 @@
         own, other = to_relative(values)
         for low, high in pieces_of(edge, width, HOP_PIECES):
             given = multiply(other, low, high)
+            own, given = lax.optimization_barrier((own, given))
             kept = lax.optimization_barrier(multiply(own, low, high))
             if marks is not None:
                 marks.append(kept)
@@ -115,6 +116,8 @@
             lined = line_exchange(jnp.broadcast_to(part[None], (half_count,) + part.shape))
             lined = lined.reshape(-1, part.shape[1])
             arrived = swap(lined, "dp")
+            if own_total is not None:
+                lined, own_total = lax.optimization_barrier((lined, own_total))
             if extra is not None and low == edge:
                 everyone = from_relative(lined[:, high - low :], arrived[:, high - low :])
                 lined, arrived = lined[:, : high - low], arrived[:, : high - low]

time: 802 us -> 802 us (level)
    ppermute x35, waiting for transfers between devices: 227 us -> 237 us  [swap(): return lax.ppermute(value, axis, [(i, i ^ step) for i in range(count)])]
  transfers between devices with their start and end apart: 53 -> 53, of which waited for: 31 -> 32; matrix products, arithmetic and copies ran while one was open for 24% -> 23% of each run, Pallas kernels for 0% -> 0%
where the time goes in v3:
time: 802 us; the launch traced here: 792 us
  waiting for transfers between devices  379 us (47%)
  matrix products  137 us (17%)
  blocking collectives  96.5 us (12%)
  starting transfers between devices  78.9 us (10%)
  local copies, waits for them, and re-layouts  42.3 us (5%)
  other arithmetic  41 us (5%)
  between operations  15.4 us (2%)
    ppermute x35, waiting for transfers between devices, swap(): return lax.ppermute(value, axis, [(i, i ^ step) for i in range(count)])  237 us
    all_to_all x10, waiting for transfers between devices, line_exchange(): lax.all_to_all(value, 'dp', split_axis=0, concat_axis=0, tiled=True, axis...  130 us
    all_to_all x2, blocking collectives, line_exchange(): lax.all_to_all(value, 'dp', split_axis=0, concat_axis=0, tiled=True, axis...  78.4 us
    dot_general x18, matrix products, product(): return jnp.dot(left, right, preferred_element_type=F32).astype(BF16)  72.3 us
    dot_general x12, matrix products, contract_last(): lax.dot_general(left, right, (((1,), (1,)), ((), ())), preferred_element_...  65 us
    all_to_all x10, starting transfers between devices, line_exchange(): lax.all_to_all(value, 'dp', split_axis=0, concat_axis=0, tiled=True, axis...  38.8 us
    ppermute x35, starting transfers between devices, swap(): return lax.ppermute(value, axis, [(i, i ^ step) for i in range(count)])  29.5 us
    dynamic_slice x3, local copies, waits for them, and re-layouts, other_half(): given = lax.dynamic_slice_in_dim(weight, (1 - position) * half, half, 1)  23 us
  transfers between devices with their start and end apart: 53, of which 32 were waited for; matrix products, arithmetic and copies ran while one was open for 23% of the time, Pallas kernels for 0%

profile of v3, /device:TPU:0, one launch (start us, length us, event | category | flops | bytes accessed | tf_op | source)
XLA Modules:
  0.0 791.6 jit_solution(1050727926154850973)
XLA Ops:
  7.2 7.6 dynamic-slice_bitcast_fusion.2
  22.9 18.2 %all_to_all.111 = bf16[32,8,640]{2,0,1:T(8,128)(2,1)S(1)} all-to-all(bf16[32,8,640]{2,0,1:T(8,128)(2,1)S(1)} %bitcast.197), channel_id=1, replica_groups=mesh['segment'=2,'dp'=8,'tensor'=2] {'dp'}, dimensions={1} | all-to-all | bytes 655360 | tf_op jit(solution)/shard_map/all_to_all | solution.py:224
  44.4 8.2 %conditional.48 = (bf16[256,6912]{1,0:T(8,128)(2,1)}) conditional(s32[]{:T(128)} %convert_element_type.494, (bf16[256,640]{1,0:T(8,128)(2,1)S(1)}, bf16[640,6912]{1,0:T(8,128)(2,1)}) %tuple.256, (bf16[640,13824]{1,0:T(8,128)(2,1)}, bf16[256,640]{1,0:T(8,128)(2,1)S(1)}) %tuple.423), branch_computations={%region_0.1_spmd, %region_1.2_spmd} | conditional | flops 2264924160 | bytes 12713992
  44.4 8.2 %fusion = bf16[256,6912]{1,0:T(8,128)(2,1)} fusion(bf16[256,640]{1,0:T(8,128)(2,1)S(1)} %get-tuple-element.368, bf16[640,13824]{1,0:T(8,128)(2,1)} %get-tuple-element.369), kind=kOutput, calls=%fused_computation | convolution fusion | flops 2264924160 | bytes 12713984 | tf_op jit(solution)/shard_map/cond/branch_1_fun/dot_general | solution.py:41
  68.4 8.0 %dynamic-slice_bitcast_fusion = bf16[640,6912]{1,0:T(8,128)(2,1)} fusion(bf16[1,640,13824]{2,1,0:T(8,128)(2,1)} %param.71, s32[]{:T(128)S(6)} %select_n.192), kind=kLoop, calls=%fused_computation.108 | loop fusion | bytes 17694724 | tf_op jit(solution)/shard_map/dynamic_slice | solution.py:184
  78.6 28.2 %collective-permute-done.8 = bf16[128,3456]{1,0:T(8,128)(2,1)S(1)} collective-permute-done((bf16[128,3456]{1,0:T(8,128)(2,1)}, bf16[128,3456]{1,0:T(8,128)(2,1)S(1)}, u32[]{:S(2)}, u32[]{:S(2)}) %collective-permute-start.8) | collective-permute-done | bytes 884768 | tf_op jit(solution)/shard_map/ppermute | solution.py:46
  112.9 18.6 %collective-permute-done.7 = bf16[128,3456]{1,0:T(8,128)(2,1)S(1)} collective-permute-done((bf16[128,3456]{1,0:T(8,128)(2,1)}, bf16[128,3456]{1,0:T(8,128)(2,1)S(1)}, u32[]{:S(2)}, u32[]{:S(2)}) %collective-permute-start.7) | collective-permute-done | bytes 884768 | tf_op jit(solution)/shard_map/ppermute | solution.py:46
  133.9 12.5 %all-to-all-done.2 = bf16[4,32,3456]{2,1,0:T(8,128)(2,1)S(1)} async-done(((bf16[4,32,3456]{2,1,0:T(8,128)(2,1)}), bf16[4,32,3456]{2,1,0:T(8,128)(2,1)S(1)}, u32[]{:S(2)}, u32[]{:S(2)}) %all-to-all-start.2) | async-done | bytes 884768 | tf_op jit(solution)/shard_map/all_to_all | solution.py:52
  186.1 19.1 %collective-permute-done.13 = bf16[128,3456]{1,0:T(8,128)(2,1)S(1)} collective-permute-done((bf16[128,3456]{1,0:T(8,128)(2,1)}, bf16[128,3456]{1,0:T(8,128)(2,1)S(1)}, u32[]{:S(2)}, u32[]{:S(2)}) %collective-permute-start.13) | collective-permute-done | bytes 884768 | tf_op jit(solution)/shard_map/ppermute | solution.py:46
  215.7 25.4 %collective-permute-done.12 = bf16[128,3456]{1,0:T(8,128)(2,1)S(1)} collective-permute-done((bf16[128,3456]{1,0:T(8,128)(2,1)}, bf16[128,3456]{1,0:T(8,128)(2,1)S(1)}, u32[]{:S(2)}, u32[]{:S(2)}) %collective-permute-start.12) | collective-permute-done | bytes 884768 | tf_op jit(solution)/shard_map/ppermute | solution.py:46
  254.4 7.7 conditional.53
  254.6 7.5 fusion.18
  263.8 8.7 %all-to-all-done.3 = bf16[4,32,3456]{2,1,0:T(8,128)(2,1)S(1)} async-done(((bf16[4,32,3456]{2,1,0:T(8,128)(2,1)}), bf16[4,32,3456]{2,1,0:T(8,128)(2,1)S(1)}, u32[]{:S(2)}, u32[]{:S(2)}) %all-to-all-start.3) | async-done | bytes 884768 | tf_op jit(solution)/shard_map/all_to_all | solution.py:52
  282.5 7.9 conditional.112
  282.5 7.9 fusion.164
  307.3 22.8 %collective-permute-done.18 = bf16[128,3456]{1,0:T(8,128)(2,1)S(1)} collective-permute-done((bf16[128,3456]{1,0:T(8,128)(2,1)}, bf16[128,3456]{1,0:T(8,128)(2,1)S(1)}, u32[]{:S(2)}, u32[]{:S(2)}) %collective-permute-start.18) | collective-permute-done | bytes 884768 | tf_op jit(solution)/shard_map/ppermute | solution.py:46
  340.2 17.0 %collective-permute-done.17 = bf16[128,3456]{1,0:T(8,128)(2,1)S(1)} collective-permute-done((bf16[128,3456]{1,0:T(8,128)(2,1)}, bf16[128,3456]{1,0:T(8,128)(2,1)S(1)}, u32[]{:S(2)}, u32[]{:S(2)}) %collective-permute-start.17) | collective-permute-done | bytes 884768 | tf_op jit(solution)/shard_map/ppermute | solution.py:46
  368.6 18.3 %collective-permute-done.15 = f32[256]{0:T(256)S(1)} collective-permute-done((f32[256]{0:T(256)S(1)}, f32[256]{0:T(256)S(1)}, u32[]{:S(2)}, u32[]{:S(2)}) %collective-permute-start.15) | collective-permute-done | bytes 1056 | tf_op jit(solution)/shard_map/ppermute | solution.py:46
  389.8 8.1 %collective-permute-done.16 = f32[256]{0:T(256)S(1)} collective-permute-done((f32[256]{0:T(256)S(1)}, f32[256]{0:T(256)S(1)}, u32[]{:S(2)}, u32[]{:S(2)}) %collective-permute-start.16) | collective-permute-done | bytes 1056 | tf_op jit(solution)/shard_map/ppermute | solution.py:46
  402.5 39.3 %all_to_all.112 = bf16[4,32,3584]{2,1,0:T(8,128)(2,1)S(1)} all-to-all(bf16[4,32,3584]{2,1,0:T(8,128)(2,1)S(1)} %broadcast_in_dim.14), channel_id=1, replica_groups={{0,4,8,12},{2,6,10,14},{1,5,9,13},{3,7,11,15},{16,20,24,28},{18,22,26,3..., dimensions={0} | all-to-all | bytes 1835008 | tf_op jit(solution)/shard_map/all_to_all | solution.py:52
  447.2 38.7 %all-to-all-done.8 = bf16[4,32,3456]{2,1,0:T(8,128)(2,1)} async-done(((bf16[4,32,3456]{2,1,0:T(8,128)(2,1)}), bf16[4,32,3456]{2,1,0:T(8,128)(2,1)}, u32[]{:S(2)}, u32[]{:S(2)}) %all-to-all-start.8) | async-done | bytes 884768 | tf_op jit(solution)/shard_map/all_to_all | solution.py:52
  501.5 8.1 %conditional.121 = (f32[256,640]{1,0:T(8,128)S(1)}) conditional(s32[]{:T(128)} %convert_element_type.494, (bf16[640,13824]{1,0:T(8,128)(2,1)}, bf16[256,6912]{1,0:T(8,128)(2,1)}) %tuple.425, (bf16[256,6912]{1,0:T(8,128)(2,1)}, bf16[640,6912]{1,0:T(8,128)(2,1)}) %tuple.298), branch_computations={%region_49.50_spmd, %region_50.51_spmd} | conditional | flops 2264924160 | bytes 13041672 | solution.py:194
  501.7 7.9 fusion.166
  542.9 25.6 %collective-permute-done.28 = bf16[128,3456]{1,0:T(8,128)(2,1)S(1)} collective-permute-done((bf16[128,3456]{1,0:T(8,128)(2,1)}, bf16[128,3456]{1,0:T(8,128)(2,1)S(1)}, u32[]{:S(2)}, u32[]{:S(2)}) %collective-permute-start.28) | collective-permute-done | bytes 884768 | tf_op jit(solution)/shard_map/ppermute | solution.py:46
  589.4 7.6 all-to-all-done.11
  601.5 20.7 %all-to-all-done.10 = bf16[4,32,3456]{2,1,0:T(8,128)(2,1)S(1)} async-done(((bf16[4,32,3456]{2,1,0:T(8,128)(2,1)}), bf16[4,32,3456]{2,1,0:T(8,128)(2,1)S(1)}, u32[]{:S(2)}, u32[]{:S(2)}) %all-to-all-start.10) | async-done | bytes 884768 | tf_op jit(solution)/shard_map/all_to_all | solution.py:52
  625.3 39.0 %all_to_all.113 = bf16[4,32,3584]{2,1,0:T(8,128)(2,1)S(1)} all-to-all(bf16[4,32,3584]{2,1,0:T(8,128)(2,1)S(1)} %broadcast_in_dim.16), channel_id=1, replica_groups={{0,4,8,12},{2,6,10,14},{1,5,9,13},{3,7,11,15},{16,20,24,28},{18,22,26,3..., dimensions={0} | all-to-all | bytes 1835008 | tf_op jit(solution)/shard_map/all_to_all | solution.py:52
  669.7 7.5 conditional.117
  669.7 7.5 fusion.165
  677.9 36.5 %all-to-all-done.12 = bf16[4,32,3456]{2,1,0:T(8,128)(2,1)} async-done(((bf16[4,32,3456]{2,1,0:T(8,128)(2,1)}), bf16[4,32,3456]{2,1,0:T(8,128)(2,1)}, u32[]{:S(2)}, u32[]{:S(2)}) %all-to-all-start.12) | async-done | bytes 884768 | tf_op jit(solution)/shard_map/all_to_all | solution.py:52
  741.0 7.5 conditional.130
  774.6 8.7 %all-to-all-done.14 = bf16[8,32,640]{2,1,0:T(8,128)(2,1)S(1)} async-done(((bf16[8,32,640]{2,1,0:T(8,128)(2,1)}), bf16[8,32,640]{2,1,0:T(8,128)(2,1)S(1)}, u32[]{:S(2)}, u32[]{:S(2)}) %all-to-all-start.14) | async-done | bytes 327712 | tf_op jit(solution)/shard_map/all_to_all | solution.py:215
  (286 shorter events, 398.7 us)
Async XLA Ops:
  7.2 161.4 %reduce-scatter.3.cloned.1.call-start = ((), (), s32[]{:S(2)}) async-start(), calls=%async_computation.17 | async-start | bytes 3981312 | tf_op jit(solution)/shard_map/reduce_scatter | solution.py:89
  14.8 29.3 %collective-permute-start.2 = (bf16[640,6912]{1,0:T(8,128)(2,1)}, bf16[640,6912]{1,0:T(8,128)(2,1)}, u32[]{:S(2)}, u32[]{:S(2)}) collective-permute-start(bf16[640,6912]{1,0:T(8,128)(2,1)} %dynamic-slice_bitcast_fusion.2), channel_id=1, source_target_pairs={{0,16},{16,0},{1,17},{17,1},{2,18},{18,2},{3,19},{19,3},{4,20},{20... | collective-permute-start | bytes 26542088 | tf_op jit(solution)/shard_map/ppermute | solution.py:46
  22.7 29.9 %collective-permute-start.6 = (bf16[640,6912]{1,0:T(8,128)(2,1)}, bf16[640,6912]{1,0:T(8,128)(2,1)}, u32[]{:S(2)}, u32[]{:S(2)}) collective-permute-start(bf16[640,6912]{1,0:T(8,128)(2,1)} %dynamic-slice_bitcast_fusion.1), channel_id=1, source_target_pairs={{0,16},{16,0},{1,17},{17,1},{2,18},{18,2},{3,19},{19,3},{4,20},{20... | collective-permute-start | bytes 26542088 | tf_op jit(solution)/shard_map/ppermute | solution.py:46
  76.3 95.2 %collective-permute-start.9 = (bf16[640,6912]{1,0:T(8,128)(2,1)}, bf16[640,6912]{1,0:T(8,128)(2,1)}, u32[]{:S(2)}, u32[]{:S(2)}) collective-permute-start(bf16[640,6912]{1,0:T(8,128)(2,1)} %dynamic-slice_bitcast_fusion), channel_id=1, source_target_pairs={{0,16},{16,0},{1,17},{17,1},{2,18},{18,2},{3,19},{19,3},{4,20},{20... | collective-permute-start | bytes 26542088 | tf_op jit(solution)/shard_map/ppermute | solution.py:46
  76.6 30.2 %collective-permute-start.8 = (bf16[128,3456]{1,0:T(8,128)(2,1)}, bf16[128,3456]{1,0:T(8,128)(2,1)S(1)}, u32[]{:S(2)}, u32[]{:S(2)}) collective-permute-start(bf16[128,3456]{1,0:T(8,128)(2,1)} %copy-done.21), channel_id=1, source_target_pairs={{0,2},{2,0},{4,6},{6,4},{8,10},{10,8},{12,14},{14,12},{1,3},{3,1},... | collective-permute-start | bytes 2654216 | tf_op jit(solution)/shard_map/ppermute | solution.py:46
  78.1 53.5 %collective-permute-start.7 = (bf16[128,3456]{1,0:T(8,128)(2,1)}, bf16[128,3456]{1,0:T(8,128)(2,1)S(1)}, u32[]{:S(2)}, u32[]{:S(2)}) collective-permute-start(bf16[128,3456]{1,0:T(8,128)(2,1)} %copy-done.20), channel_id=1, source_target_pairs={{0,2},{2,0},{4,6},{6,4},{8,10},{10,8},{12,14},{14,12},{1,3},{3,1},... | collective-permute-start | bytes 2654216 | tf_op jit(solution)/shard_map/ppermute | solution.py:46
  109.1 37.3 %all-to-all-start.2 = ((bf16[4,32,3456]{2,1,0:T(8,128)(2,1)}), bf16[4,32,3456]{2,1,0:T(8,128)(2,1)S(1)}, u32[]{:S(2)}, u32[]{:S(2)}) async-start(bf16[4,32,3456]{2,1,0:T(8,128)(2,1)} %bitcast.11), calls=%async_computation.3 | async-start | bytes 1769472 | tf_op jit(solution)/shard_map/all_to_all | solution.py:52
  149.9 104.5 %all-gather.5.cloned.1.call-start = ((), (), s32[]{:S(2)}) async-start(), calls=%async_computation.18 | async-start | bytes 3981312 | tf_op jit(solution)/shard_map/all_gather | solution.py:135
  180.1 25.1 %collective-permute-start.13 = (bf16[128,3456]{1,0:T(8,128)(2,1)}, bf16[128,3456]{1,0:T(8,128)(2,1)S(1)}, u32[]{:S(2)}, u32[]{:S(2)}) collective-permute-start(bf16[128,3456]{1,0:T(8,128)(2,1)} %get-tuple-element.583), channel_id=1, source_target_pairs={{0,2},{2,0},{4,6},{6,4},{8,10},{10,8},{12,14},{14,12},{1,3},{3,1},... | collective-permute-start | bytes 2654216 | tf_op jit(solution)/shard_map/ppermute | solution.py:46
  184.1 57.0 %collective-permute-start.12 = (bf16[128,3456]{1,0:T(8,128)(2,1)}, bf16[128,3456]{1,0:T(8,128)(2,1)S(1)}, u32[]{:S(2)}, u32[]{:S(2)}) collective-permute-start(bf16[128,3456]{1,0:T(8,128)(2,1)} %copy-done.22), channel_id=1, source_target_pairs={{0,2},{2,0},{4,6},{6,4},{8,10},{10,8},{12,14},{14,12},{1,3},{3,1},... | collective-permute-start | bytes 2654216 | tf_op jit(solution)/shard_map/ppermute | solution.py:46
  207.5 41.5 %all-to-all-start.4 = ((bf16[4,32,3456]{2,1,0:T(8,128)(2,1)}), bf16[4,32,3456]{2,1,0:T(8,128)(2,1)S(1)}, u32[]{:S(2)}, u32[]{:S(2)}) async-start(bf16[4,32,3456]{2,1,0:T(8,128)(2,1)} %bitcast.18), calls=%async_computation.5 | async-start | bytes 1769472 | tf_op jit(solution)/shard_map/all_to_all | solution.py:52
  249.0 23.5 %all-to-all-start.3 = ((bf16[4,32,3456]{2,1,0:T(8,128)(2,1)}), bf16[4,32,3456]{2,1,0:T(8,128)(2,1)S(1)}, u32[]{:S(2)}, u32[]{:S(2)}) async-start(bf16[4,32,3456]{2,1,0:T(8,128)(2,1)} %bitcast.183), calls=%async_computation.4 | async-start | bytes 1769472 | tf_op jit(solution)/shard_map/all_to_all | solution.py:52
  252.5 146.5 %reduce-scatter.5.cloned.1.call-start = ((), (), s32[]{:S(2)}) async-start(), calls=%async_computation.19 | async-start | bytes 3981312 | tf_op jit(solution)/shard_map/reduce_scatter | solution.py:89
  298.6 31.5 %collective-permute-start.18 = (bf16[128,3456]{1,0:T(8,128)(2,1)}, bf16[128,3456]{1,0:T(8,128)(2,1)S(1)}, u32[]{:S(2)}, u32[]{:S(2)}) collective-permute-start(bf16[128,3456]{1,0:T(8,128)(2,1)} %get-tuple-element.588), channel_id=1, source_target_pairs={{0,2},{2,0},{4,6},{6,4},{8,10},{10,8},{12,14},{14,12},{1,3},{3,1},... | collective-permute-start | bytes 2654216 | tf_op jit(solution)/shard_map/ppermute | solution.py:46
  307.3 49.9 %collective-permute-start.17 = (bf16[128,3456]{1,0:T(8,128)(2,1)}, bf16[128,3456]{1,0:T(8,128)(2,1)S(1)}, u32[]{:S(2)}, u32[]{:S(2)}) collective-permute-start(bf16[128,3456]{1,0:T(8,128)(2,1)} %copy-done.23), channel_id=1, source_target_pairs={{0,2},{2,0},{4,6},{6,4},{8,10},{10,8},{12,14},{14,12},{1,3},{3,1},... | collective-permute-start | bytes 2654216 | tf_op jit(solution)/shard_map/ppermute | solution.py:46
  332.4 27.1 %all-to-all-start.6 = ((bf16[4,32,3456]{2,1,0:T(8,128)(2,1)}), bf16[4,32,3456]{2,1,0:T(8,128)(2,1)S(1)}, u32[]{:S(2)}, u32[]{:S(2)}) async-start(bf16[4,32,3456]{2,1,0:T(8,128)(2,1)} %bitcast.23), calls=%async_computation.8 | async-start | bytes 1769472 | tf_op jit(solution)/shard_map/all_to_all | solution.py:52
  359.5 39.4 %all-to-all-start.5 = ((bf16[4,32,3456]{2,1,0:T(8,128)(2,1)}), bf16[4,32,3456]{2,1,0:T(8,128)(2,1)S(1)}, u32[]{:S(2)}, u32[]{:S(2)}) async-start(bf16[4,32,3456]{2,1,0:T(8,128)(2,1)} %bitcast.182), calls=%async_computation.7 | async-start | bytes 1769472 | tf_op jit(solution)/shard_map/all_to_all | solution.py:52
  363.0 138.5 %all-gather.9.cloned.1.call-start = ((), (), s32[]{:S(2)}) async-start(), calls=%async_computation.21 | async-start | bytes 3981312 | tf_op jit(solution)/shard_map/all_gather | solution.py:135
  442.8 43.1 %all-to-all-start.8 = ((bf16[4,32,3456]{2,1,0:T(8,128)(2,1)}), bf16[4,32,3456]{2,1,0:T(8,128)(2,1)}, u32[]{:S(2)}, u32[]{:S(2)}) async-start(bf16[4,32,3456]{2,1,0:T(8,128)(2,1)} %broadcast_in_dim.13), calls=%async_computation.10 | async-start | bytes 1769472 | tf_op jit(solution)/shard_map/all_to_all | solution.py:52
  447.1 222.6 %all-gather.7.cloned.1.call-start = ((), (), s32[]{:S(2)}) async-start(), calls=%async_computation.20 | async-start | bytes 3981312 | tf_op jit(solution)/shard_map/all_gather | solution.py:135
  447.2 49.0 %collective-permute-start.21 = (bf16[128,3584]{1,0:T(8,128)(2,1)S(1)}, bf16[128,3584]{1,0:T(8,128)(2,1)S(1)}, u32[]{:S(2)}, u32[]{:S(2)}) collective-permute-start(bf16[128,3584]{1,0:T(8,128)(2,1)S(1)} %bitcast.178), channel_id=1, source_target_pairs={{0,2},{2,0},{4,6},{6,4},{8,10},{10,8},{12,14},{14,12},{1,3},{3,1},... | collective-permute-start | bytes 2752520 | tf_op jit(solution)/shard_map/ppermute | solution.py:46
  486.0 23.6 %collective-permute-start.22 = (bf16[128,3456]{1,0:T(8,128)(2,1)}, bf16[128,3456]{1,0:T(8,128)(2,1)}, u32[]{:S(2)}, u32[]{:S(2)}) collective-permute-start(bf16[128,3456]{1,0:T(8,128)(2,1)} %bitcast.26), channel_id=1, source_target_pairs={{0,2},{2,0},{4,6},{6,4},{8,10},{10,8},{12,14},{14,12},{1,3},{3,1},... | collective-permute-start | bytes 2654216 | tf_op jit(solution)/shard_map/ppermute | solution.py:46
  536.8 31.7 %collective-permute-start.28 = (bf16[128,3456]{1,0:T(8,128)(2,1)}, bf16[128,3456]{1,0:T(8,128)(2,1)S(1)}, u32[]{:S(2)}, u32[]{:S(2)}) collective-permute-start(bf16[128,3456]{1,0:T(8,128)(2,1)} %get-tuple-element.598), channel_id=1, source_target_pairs={{0,2},{2,0},{4,6},{6,4},{8,10},{10,8},{12,14},{14,12},{1,3},{3,1},... | collective-permute-start | bytes 2654216 | tf_op jit(solution)/shard_map/ppermute | solution.py:46
  542.1 44.9 %collective-permute-start.27 = (bf16[128,3456]{1,0:T(8,128)(2,1)}, bf16[128,3456]{1,0:T(8,128)(2,1)S(1)}, u32[]{:S(2)}, u32[]{:S(2)}) collective-permute-start(bf16[128,3456]{1,0:T(8,128)(2,1)} %copy-done.24), channel_id=1, source_target_pairs={{0,2},{2,0},{4,6},{6,4},{8,10},{10,8},{12,14},{14,12},{1,3},{3,1},... | collective-permute-start | bytes 2654216 | tf_op jit(solution)/shard_map/ppermute | solution.py:46
  570.8 26.2 %all-to-all-start.11 = ((bf16[4,32,3456]{2,1,0:T(8,128)(2,1)}), bf16[4,32,3456]{2,1,0:T(8,128)(2,1)S(1)}, u32[]{:S(2)}, u32[]{:S(2)}) async-start(bf16[4,32,3456]{2,1,0:T(8,128)(2,1)} %bitcast.39), calls=%async_computation.13 | async-start | bytes 1769472 | tf_op jit(solution)/shard_map/all_to_all | solution.py:52
  597.0 25.2 %all-to-all-start.10 = ((bf16[4,32,3456]{2,1,0:T(8,128)(2,1)}), bf16[4,32,3456]{2,1,0:T(8,128)(2,1)S(1)}, u32[]{:S(2)}, u32[]{:S(2)}) async-start(bf16[4,32,3456]{2,1,0:T(8,128)(2,1)} %bitcast.184), calls=%async_computation.12 | async-start | bytes 1769472 | tf_op jit(solution)/shard_map/all_to_all | solution.py:52
  600.5 139.8 %all-gather.11.cloned.1.call-start = ((), (), s32[]{:S(2)}) async-start(), calls=%async_computation.22 | async-start | bytes 3981312 | tf_op jit(solution)/shard_map/all_gather | solution.py:135
  665.4 49.0 %all-to-all-start.12 = ((bf16[4,32,3456]{2,1,0:T(8,128)(2,1)}), bf16[4,32,3456]{2,1,0:T(8,128)(2,1)}, u32[]{:S(2)}, u32[]{:S(2)}) async-start(bf16[4,32,3456]{2,1,0:T(8,128)(2,1)} %broadcast_in_dim.15), calls=%async_computation.14 | async-start | bytes 1769472 | tf_op jit(solution)/shard_map/all_to_all | solution.py:52
  677.2 37.2 %collective-permute-start.19 = (bf16[256,640]{1,0:T(8,128)(2,1)S(1)}, bf16[256,640]{1,0:T(8,128)(2,1)S(1)}, u32[]{:S(2)}, u32[]{:S(2)}) collective-permute-start(bf16[256,640]{1,0:T(8,128)(2,1)S(1)} %get-tuple-element.590), channel_id=1, source_target_pairs={{0,16},{16,0},{1,17},{17,1},{2,18},{18,2},{3,19},{19,3},{4,20},{20... | collective-permute-start | bytes 983048 | tf_op jit(solution)/shard_map/ppermute | solution.py:46
  677.3 58.3 %collective-permute-start.29 = (bf16[128,3584]{1,0:T(8,128)(2,1)S(1)}, bf16[128,3584]{1,0:T(8,128)(2,1)S(1)}, u32[]{:S(2)}, u32[]{:S(2)}) collective-permute-start(bf16[128,3584]{1,0:T(8,128)(2,1)S(1)} %bitcast.175), channel_id=1, source_target_pairs={{0,2},{2,0},{4,6},{6,4},{8,10},{10,8},{12,14},{14,12},{1,3},{3,1},... | collective-permute-start | bytes 2752520 | tf_op jit(solution)/shard_map/ppermute | solution.py:46
  714.4 34.1 %collective-permute-start.30 = (bf16[128,3456]{1,0:T(8,128)(2,1)}, bf16[128,3456]{1,0:T(8,128)(2,1)}, u32[]{:S(2)}, u32[]{:S(2)}) collective-permute-start(bf16[128,3456]{1,0:T(8,128)(2,1)} %bitcast.40), channel_id=1, source_target_pairs={{0,2},{2,0},{4,6},{6,4},{8,10},{10,8},{12,14},{14,12},{1,3},{3,1},... | collective-permute-start | bytes 2654216 | tf_op jit(solution)/shard_map/ppermute | solution.py:46
  722.7 44.9 %all-to-all-start.7 = ((bf16[8,32,640]{2,1,0:T(8,128)(2,1)}), bf16[8,32,640]{2,1,0:T(8,128)(2,1)S(1)}, u32[]{:S(2)}, u32[]{:S(2)}) async-start(bf16[8,32,640]{2,1,0:T(8,128)(2,1)} %bitcast.24), calls=%async_computation.9 | async-start | bytes 655360 | tf_op jit(solution)/shard_map/all_to_all | solution.py:215
  (46 other events, 254.4 us)
Sparse Core Ops, SparseCore 0:
  52.7 98.1 reduce-scatter.2
  170.8 83.4 all-gather.4
  290.5 107.7 reduce-scatter.4
  402.4 93.6 all-gather.8
  498.1 77.1 all-gather.6
  625.2 93.1 all-gather.10
